TPU v7x, 1024 devices: a whole 4x8x16 slice. The times are simulated.
1024 devices in a mesh: occ: 64 (over z_hi, x, y), vir: 16 (over z_lo, core).
Axes of the slice: x: 4, y: 8, z: 16 (z_hi: 2, z_lo: 8; z = z_hi * 8 + z_lo), core: 2. Of those that a mesh axis runs over, the one named last changes fastest.
Arguments:
- amplitudes: float32 [65536, 4096], P('occ', 'vir'), may hold values from -6 to 6
- integrals: float32 [4096, 4096], P('vir'), may hold values from -0.25 to 0.25
- occ_irrep: int32 [256], replicated, may hold values from 0 to 7
- vir_irrep: int32 [64], replicated, may hold values from 0 to 7, as said below
- tile_map: int32 [64, 32], P('occ', 'vir'), may hold values 0 or 1
Outputs:
- residual: float32 [65536, 4096], P('occ', 'vir')
Inputs may be any that keep to these rules, and one draw needn't show every extreme that they name: `vir_irrep`: each irrep labels exactly 8 of the virtual orbitals.
All inputs are finite; a program needn't handle non-finite values. No bound on the sum of `tile_map` on one device may be relied on, other than what follows from the above.
Results may differ from a plain program's by a relative error of at most 0.000073.
Values sent between devices are 32-bit elements; how exact they have to be, the bound alone decides.
No kernel may reach another device: no remote copies, remote signals or barrier semaphores. Data moves between devices by JAX's collectives and lax.ppermute only.
A program may use at most 64 MiB of HBM per device.

v0:
```python
import jax
import jax.numpy as jnp
from jax import lax
from jax.sharding import PartitionSpec as P


def mirror_rows(block, occ_width, nocc):
    cols = block.shape[1]
    three = block.reshape(occ_width, nocc, cols)
    got = lax.all_to_all(three, "occ", split_axis=1, concat_axis=0, tiled=True)
    return got.transpose(1, 0, 2).reshape(occ_width * nocc, cols)


def mirror_cols(block, nvir):
    rows = block.shape[0]
    three = block.reshape(rows, block.shape[1] // nvir, nvir)
    got = lax.all_to_all(three, "vir", split_axis=2, concat_axis=1, tiled=True)
    return got.transpose(0, 2, 1).reshape(rows, block.shape[1])


def body(amplitudes, integrals, occ_irrep, vir_irrep, tile_map):
    nocc = occ_irrep.shape[0]
    nvir = vir_irrep.shape[0]
    rows = amplitudes.shape[0]
    occ_width = rows // nocc
    cd_local = amplitudes.shape[1]
    vir_width = cd_local // nvir
    occ_pos = lax.axis_index("occ")
    vir_pos = lax.axis_index("vir")
    mine_i = lax.dynamic_slice_in_dim(occ_irrep, occ_pos * occ_width, occ_width, 0)
    mine_c = lax.dynamic_slice_in_dim(vir_irrep, vir_pos * vir_width, vir_width, 0)
    sym_rows = jnp.bitwise_xor(mine_i[:, None], occ_irrep[None, :]).reshape(-1)
    sym_local = jnp.bitwise_xor(mine_c[:, None], vir_irrep[None, :]).reshape(-1)
    sym_every = jnp.bitwise_xor(vir_irrep[:, None], vir_irrep[None, :]).reshape(-1)
    tiles = jnp.repeat(tile_map[0], cd_local // tile_map.shape[1])
    keep = jnp.logical_and(sym_rows[:, None] == sym_local[None, :], tiles[None, :] == 1)
    amps = jnp.where(keep, amplitudes, jnp.float32(0.0))
    panel = jnp.where(sym_local[:, None] == sym_every[None, :], integrals, jnp.float32(0.0))
    partial_sum = jnp.dot(
        amps, panel, precision=lax.Precision.HIGHEST, preferred_element_type=jnp.float32
    )
    summed = lax.psum_scatter(partial_sum, "vir", scatter_dimension=1, tiled=True)
    summed = summed - mirror_cols(summed, nvir)
    summed = summed - mirror_rows(summed, occ_width, nocc)
    return summed


def solution(mesh):
    placed = (P("occ", "vir"), P("vir", None), P(), P(), P("occ", "vir"))
    return jax.shard_map(
        body, mesh=mesh, in_specs=placed, out_specs=P("occ", "vir"), check_vma=False
    )
```

profile of v0, /device:TPU:70, one launch (start us, length us, event | category | flops | bytes accessed | tf_op | source)
XLA Modules:
  0.0 382.1 jit_solution(11339477576708564677)
XLA Ops:
  6.5 0.0 reduce-scatter.2.cloned.1.call-start
  6.5 0.8 broadcast_xor_fusion
  7.3 0.7 dynamic_slice.7
  8.1 0.7 compare_bitcast_fusion
  8.7 0.1 broadcast_bitcast_fusion
  8.8 0.7 broadcast_xor_fusion.1
  9.5 0.1 xor.71
  9.6 0.8 dynamic_slice.6
  10.4 0.7 xor_bitcast_fusion
  11.1 0.1 xor.75
  11.2 18.3 %fusion = f32[1024,4096]{1,0:T(8,128)} fusion(f32[256,4096]{1,0:T(8,128)} %param.6, s32[4096]{0:T(1024)S(1)} %xor.75, s32[256]{0:T(256)S(1)} %xor.71, f32[1024,256]{1,0:T(8,128)} %param.5, s32[1024]{0:T(1024)S(1)} %bitcast.31, pred[256]{0:T(512)(128)(4,1)S(1)} %broadcast_bitcast_fusion), kind=kOutput, calls=%fused_computation | convolution fusion | flops 12887785472 | bytes 22041856 | tf_op jit(solution)/shard_map/dot_general | solution.py:39
  29.5 0.0 reduce-scatter.2.cloned.1.call-update
  29.6 194.4 %reduce-scatter.2.cloned.1.call-done = f32[1024,256]{1,0:T(8,128)} async-done(((f32[1024,4096]{1,0:T(8,128)}), f32[1024,256]{1,0:T(8,128)}) %reduce-scatter.2.cloned.1.call-update) | async-done | bytes 1048592 | tf_op jit(solution)/shard_map/reduce_scatter | solution.py:42
  223.9 1.6 copy.14
  225.5 0.7 copy.15
  226.2 0.0 copy-start
  226.2 63.3 %all_to_all.36 = f32[1024,4,64]{0,1,2:T(4,128)S(1)} all-to-all(f32[1024,4,64]{0,1,2:T(4,128)S(1)} %copy.15), channel_id=1, replica_groups=mesh['occ'=64,'vir'=16] {'vir'}, dimensions={2} | all-to-all | bytes 2097152 | tf_op jit(solution)/shard_map/all_to_all | solution.py:17
  289.5 0.7 copy.16
  290.2 0.6 copy.17
  290.8 0.3 copy.18
  291.1 0.0 copy-done
  291.1 0.1 sub.6
  291.3 0.7 copy.19
  292.0 81.7 %all_to_all.37 = f32[4,256,256]{2,0,1:T(4,128)S(1)} all-to-all(f32[4,256,256]{2,0,1:T(4,128)S(1)} %copy.19), channel_id=1, replica_groups=mesh['occ'=64,'vir'=16] {'occ'}, dimensions={1} | all-to-all | bytes 2097152 | tf_op jit(solution)/shard_map/all_to_all | solution.py:10
  373.6 0.2 copy.20
  373.8 0.4 all_to_all.33
  374.2 1.1 bitcast_subtract_fusion
  (1 shorter events, 0.0 us)
Async XLA Ops:
  6.5 217.4 %reduce-scatter.2.cloned.1.call-start = ((), (), s32[]{:S(2)}) async-start(), calls=%async_computation.3 | async-start | bytes 17825792 | tf_op jit(solution)/shard_map/reduce_scatter | solution.py:42
  226.2 64.9 %copy-start = (f32[1024,256]{1,0:T(8,128)S(1)}, f32[1024,256]{1,0:T(8,128)}, u32[]{:S(2)}) copy-start(f32[1024,256]{1,0:T(8,128)} %reduce-scatter.2.cloned.1.call-done) | copy-start | bytes 3145732
Sparse Core Ops, SparseCore 0:
  29.7 194.2 reduce-scatter.1
where the time goes:
time: 382 us
  waiting for transfers between devices  194 us (51%)
  blocking collectives  145 us (38%)
  matrix products  18.3 us (5%)
  between operations  13.5 us (4%)
  local copies, waits for them, and re-layouts  6.82 us (2%)
  other arithmetic  4.17 us (1%)
    reduce_scatter x1, waiting for transfers between devices, body(): lax.psum_scatter(partial_sum, 'vir', scatter_dimension=1, tiled=True)  194 us
    all_to_all x1, blocking collectives, mirror_rows(): got = lax.all_to_all(three, 'occ', split_axis=1, concat_axis=0, tiled=True)  81.7 us
    all_to_all x1, blocking collectives, mirror_cols(): got = lax.all_to_all(three, 'vir', split_axis=2, concat_axis=1, tiled=True)  63.3 us
    dot_general x1, matrix products, body(): jnp.dot(amps, panel, precision=lax.Precision.HIGHEST, preferred_element_t...  18.3 us
  transfers between devices with their start and end apart: 1, of which 1 were waited for; matrix products, arithmetic and copies ran while one was open for 0% of the time, Pallas kernels for 0%

commit v1 on v0

v1 whole, which is shorter than its diff:
```python
import functools

import jax
import jax.numpy as jnp
from jax import lax
from jax.experimental import pallas as pl
from jax.experimental.pallas import tpu as pltpu
from jax.sharding import PartitionSpec as P

F32, BF16, I32 = jnp.float32, jnp.bfloat16, jnp.int32
CLASSES = 8
RANKS = 8
GROUP = 4
CHUNK = 512
VMEM = 48 * 1024 * 1024


def iota(shape, dim):
    return lax.broadcasted_iota(I32, shape, dim)


def pieces(value, count):
    out = []
    for step in range(count):
        part = value.astype(BF16)
        out.append(part)
        if step + 1 < count:
            value = value - part.astype(F32)
    return out


def dot(a, b):
    return lax.dot_general(a, b, (((1,), (0,)), ((), ())), preferred_element_type=F32)


def dot_nt(a, b):
    return lax.dot_general(a, b, (((1,), (1,)), ((), ())), preferred_element_type=F32)


def to_column(row):
    n = row.shape[1]
    return jnp.sum(jnp.where(iota((n, n), 0) == iota((n, n), 1), row, 0.0), axis=1, keepdims=True)


def pick_lanes(column, index):
    shape = (column.shape[0], index.shape[1])
    return jnp.sum(jnp.where(iota(shape, 0) == index, column, 0.0), axis=0, keepdims=True)


def pick_rows(row, index):
    shape = (index.shape[0], row.shape[1])
    return jnp.sum(jnp.where(iota(shape, 1) == index, row, 0.0), axis=1, keepdims=True)


def orbitals(vir_ref):
    row = vir_ref[...].astype(F32)
    col = to_column(row)
    n = row.shape[1]
    below = jnp.logical_and(col == row, iota((n, n), 1) < iota((n, n), 0))
    rank = jnp.sum(jnp.where(below, 1.0, 0.0), axis=1, keepdims=True)
    return row, col, rank


def pair_lanes(col, first, nvir, width):
    lane = iota((1, width * nvir), 1)
    one = pick_lanes(col, first + lane // nvir).astype(I32)
    two = pick_lanes(col, lane % nvir).astype(I32)
    return jnp.bitwise_xor(one, two)


def amps_kernel(amp_ref, occ_ref, vir_ref, tile_ref, own_ref, send_ref):
    nocc, nvir = occ_ref.shape[1], vir_ref.shape[1]
    width = amp_ref.shape[1] // nvir
    oi = amp_ref.shape[0] // nocc
    o, v = lax.axis_index("occ"), lax.axis_index("vir")
    _, vcol, rank = orbitals(vir_ref)
    occ = occ_ref[...].astype(F32)
    irr_j = to_column(occ).astype(I32)
    sym_cd = pair_lanes(vcol, v * width, nvir, width)
    lane = iota((1, width * nvir), 1)
    tiles = tile_ref.shape[1]
    tile = jnp.zeros_like(lane)
    for t in range(tiles):
        tile = jnp.where(lane // (width * nvir // tiles) == t, tile_ref[0, t], tile)
    sym_cd = jnp.where(tile == 1, sym_cd, -1)
    cdr, n = width * nvir, oi * width * RANKS
    rank_rows = jnp.concatenate([rank] * width, axis=0).astype(I32)
    col = iota((cdr, n), 1)
    squeeze = jnp.logical_and((col // RANKS) % width == iota((cdr, n), 0) // nvir, col % RANKS == rank_rows)
    squeeze = jnp.where(squeeze, 1.0, 0.0).astype(BF16)
    lanes = iota((nocc, n), 1) // (width * RANKS)
    own = jnp.zeros((nocc, n), F32)
    for ii in range(oi):
        irr_i = pick_rows(occ, jnp.full((1, 1), o * oi + ii, I32)).astype(I32)
        keep = jnp.bitwise_xor(irr_j, irr_i) == sym_cd
        block = jnp.where(keep, amp_ref[ii * nocc:(ii + 1) * nocc, :], 0.0)
        short = sum(dot(part, squeeze) for part in pieces(block, 3))
        own = jnp.where(lanes == ii, short, own)
    own_ref[...] = own
    devices = nocc // oi
    lanes = iota((devices, n), 1) // (width * RANKS)
    swapped = [jnp.zeros((devices, n), F32) for _ in range(oi)]
    for jj in range(oi):
        rows = own_ref[pl.ds(jj, devices, stride=oi), :]
        for ii in range(oi):
            shift = (jj - ii) % oi * (width * RANKS)
            moved = pltpu.roll(rows, shift, 1) if shift else rows
            swapped[ii] = jnp.where(lanes == jj, moved, swapped[ii])
    for ii in range(oi):
        send_ref[pl.ds(ii, devices, stride=oi), :] = swapped[ii]


def panel_kernel(steps, int_ref, vir_ref, *refs):
    outs, total = refs[:-1], refs[-1]
    q = pl.program_id(0)
    nvir = vir_ref.shape[1]
    cdr, chunk = int_ref.shape
    width = cdr // nvir
    v = lax.axis_index("vir")
    vrow, vcol, rank = orbitals(vir_ref)
    row = iota((cdr, 1), 0)
    sym_rows = jnp.bitwise_xor(pick_rows(vrow, v * width + row // nvir).astype(I32), pick_rows(vrow, row % nvir).astype(I32))
    lane = iota((1, chunk), 1)
    a, b = q * (chunk // nvir) + lane // nvir, lane % nvir
    sym_ab = jnp.bitwise_xor(pick_lanes(vcol, a).astype(I32), pick_lanes(vcol, b).astype(I32))
    plus = a * RANKS + pick_lanes(rank, b).astype(I32)
    minus = b * RANKS + pick_lanes(rank, a).astype(I32)
    n = nvir * RANKS
    dest = n // (width * RANKS * GROUP)
    col = iota((n, 1), 0)
    to = (col // (n // GROUP)) ^ (v % GROUP)
    group = ((col // (width * RANKS)) % dest) ^ (v // GROUP)
    code = (group * GROUP + to) * (width * RANKS) + col % (width * RANKS)
    fold = jnp.where(code == plus, 1.0, 0.0) - jnp.where(code == minus, 1.0, 0.0)
    fold = fold.astype(BF16)
    block = jnp.where(sym_rows == sym_ab, int_ref[...], 0.0)
    part = sum(dot_nt(fold, piece) for piece in pieces(block, 2))

    @pl.when(q == 0)
    def _():
        total[...] = part

    @pl.when(q > 0)
    def _():
        total[...] += part

    @pl.when(q == steps - 1)
    def _():
        k = CLASSES * width * RANKS
        new = iota((cdr, k), 1)
        old = iota((cdr, k), 0)
        rank_rows = jnp.concatenate([rank] * width, axis=0).astype(I32)
        order = jnp.logical_and(new // (width * RANKS) == sym_rows, (new // RANKS) % width == old // nvir)
        order = jnp.logical_and(order, new % RANKS == rank_rows)
        order = jnp.where(order, 1.0, 0.0).astype(BF16)
        placed = sum(dot(piece, order) for piece in pieces(total[...], 2))
        rows = n // GROUP
        for k, out in enumerate(outs):
            out[...] = placed[k * rows:(k + 1) * rows, :]


def antisym_kernel(own_ref, got_ref, out_ref):
    out_ref[...] = (own_ref[...] - got_ref[...]).T


def ladder_kernel(oi, *refs):
    amps, panels, occ_ref, outs = refs[:GROUP], refs[GROUP:2 * GROUP], refs[2 * GROUP], refs[2 * GROUP + 1:]
    nocc = occ_ref.shape[1]
    o = lax.axis_index("occ")
    occ = occ_ref[...].astype(F32)
    cm = amps[0].shape[0] // oi
    stacked = []
    for ref in panels:
        high, low = pieces(ref[...], 2)
        stacked.append((jnp.concatenate([high, low], axis=0), high))
    n = panels[0].shape[0]
    for ii in range(oi):
        irr_i = pick_rows(occ, jnp.full((1, 1), o * oi + ii, I32)).astype(I32)
        sym = jnp.bitwise_xor(occ_ref[...], irr_i)
        total = jnp.zeros((n, nocc), F32)
        for ref, (both, high) in zip(amps, stacked, strict=True):
            block = ref[ii * cm:(ii + 1) * cm, :]
            spread = jnp.concatenate([jnp.where(sym == s, block, 0.0) for s in range(CLASSES)], axis=0)
            upper, lower = pieces(spread, 2)
            first = dot(both, upper)
            total = total + (first[:n, :] + (first[n:, :] + dot(high, lower)))
        for d, out in enumerate(outs):
            out[ii * cm:(ii + 1) * cm, :] = total[d * cm:(d + 1) * cm, :]


def spread_kernel(oi, *refs):
    parts, occ_ref, vir_ref, out_ref = refs[:-3], refs[-3], refs[-2], refs[-1]
    nocc, nvir = occ_ref.shape[1], vir_ref.shape[1]
    width = out_ref.shape[1] // nvir
    o, v = lax.axis_index("occ"), lax.axis_index("vir")
    _, vcol, rank = orbitals(vir_ref)
    occ = occ_ref[...].astype(F32)
    irr_j = to_column(occ).astype(I32)
    sym_ab = pair_lanes(vcol, v * width, nvir, width)
    total = parts[0][...]
    for ref in parts[1:]:
        total = total + ref[...]
    total = total.T
    split = pieces(total, 3)
    n = total.shape[1]
    lane = iota((1, width * nvir), 1)
    rank_lanes = pick_lanes(rank, lane % nvir).astype(I32)
    row = iota((n, width * nvir), 0)
    open_ = jnp.logical_and((row // RANKS) % width == lane // nvir, row % RANKS == rank_lanes)
    for ii in range(oi):
        wide = jnp.where(jnp.logical_and(open_, row // (width * RANKS) == ii), 1.0, 0.0).astype(BF16)
        full = sum(dot(part, wide) for part in split)
        irr_i = pick_rows(occ, jnp.full((1, 1), o * oi + ii, I32)).astype(I32)
        keep = jnp.bitwise_xor(irr_j, irr_i) == sym_ab
        out_ref[ii * nocc:(ii + 1) * nocc, :] = jnp.where(keep, full, 0.0)


def whole(count):
    return [pl.BlockSpec(memory_space=pltpu.VMEM)] * count


def call(kernel, outs, ins, flops, interpret, smem=()):
    specs = whole(len(ins))
    for k in smem:
        specs[k] = pl.BlockSpec(memory_space=pltpu.SMEM)
    moved = sum(x.size * 4 for x in ins) + sum(x.size * 4 for x in outs)
    return pl.pallas_call(
        kernel,
        out_shape=outs,
        in_specs=specs,
        out_specs=whole(len(outs)),
        compiler_params=pltpu.CompilerParams(vmem_limit_bytes=VMEM),
        cost_estimate=pl.CostEstimate(flops=flops, bytes_accessed=moved, transcendentals=0),
        interpret=interpret,
    )(*ins)


def array(*shape):
    return jax.ShapeDtypeStruct(shape, F32)


def body(nvirdev, interpret, amplitudes, integrals, occ_irrep, vir_irrep, tile_map):
    nocc, nvir = occ_irrep.shape[0], vir_irrep.shape[0]
    oi = amplitudes.shape[0] // nocc
    cdr = amplitudes.shape[1]
    width = cdr // nvir
    cm = width * RANKS
    n = nvir * RANKS
    occ = occ_irrep.reshape(1, nocc)
    vir = vir_irrep.reshape(1, nvir)

    def swap(x, k):
        return lax.ppermute(x, "vir", [(i, i ^ k) for i in range(nvirdev)])

    own, send = call(amps_kernel, [array(nocc, oi * cm)] * 2, [amplitudes, occ, vir, tile_map], 10**9, interpret, (3,))
    got = lax.all_to_all(send.reshape(nocc // oi, oi, oi * cm), "occ", 0, 0).reshape(nocc, oi * cm)

    steps = integrals.shape[1] // CHUNK
    k = CLASSES * cm
    panels = pl.pallas_call(
        functools.partial(panel_kernel, steps),
        grid=(steps,),
        out_shape=[array(n // GROUP, k)] * GROUP,
        in_specs=[pl.BlockSpec((cdr, CHUNK), lambda q: (0, q)), pl.BlockSpec((1, nvir), lambda q: (0, 0))],
        out_specs=[pl.BlockSpec((n // GROUP, k), lambda q: (0, 0))] * GROUP,
        scratch_shapes=[pltpu.VMEM((n, cdr), F32)],
        compiler_params=pltpu.CompilerParams(vmem_limit_bytes=VMEM, dimension_semantics=("arbitrary",)),
        cost_estimate=pl.CostEstimate(flops=4 * n * cdr * nvir * nvir, bytes_accessed=8 * integrals.size, transcendentals=0),
        interpret=interpret,
    )(integrals, vir)
    panels = [x if k == 0 else swap(x, k) for k, x in enumerate(panels)]

    (anti,) = call(antisym_kernel, [array(oi * cm, nocc)], [own, got], 10**6, interpret)
    blocks = [anti if k == 0 else swap(anti, k) for k in range(GROUP)]
    far = nvirdev // GROUP
    partial_sums = call(
        functools.partial(ladder_kernel, oi), [array(oi * cm, nocc)] * far, [*blocks, *panels, occ], 2 * 10**9, interpret
    )
    sums = [x if d == 0 else swap(x, d * GROUP) for d, x in enumerate(partial_sums)]
    (out,) = call(
        functools.partial(spread_kernel, oi), [array(*amplitudes.shape)], [*sums, occ, vir], 10**9, interpret
    )
    return out


def solution(mesh, interpret=False):
    placed = (P("occ", "vir"), P("vir", None), P(), P(), P("occ", "vir"))
    return jax.shard_map(
        functools.partial(body, mesh.shape["vir"], interpret),
        mesh=mesh,
        in_specs=placed,
        out_specs=P("occ", "vir"),
        check_vma=False,
    )
```

time: 382 us -> 99.6 us (0.26)
  the two profiles are of different devices: /device:TPU:70 before, /device:TPU:8 now
where the time goes in v1:
time: 99.6 us; the launch traced here: 99.1 us
  starting transfers between devices  56.6 us (57%)
  waiting for transfers between devices  24 us (24%)
  Pallas kernels  12.2 us (12%)
  local copies, waits for them, and re-layouts  6.06 us (6%)
    ppermute x9, starting transfers between devices, swap(): return lax.ppermute(x, 'vir', [(i, i ^ k) for i in range(nvirdev)])  29.2 us
    all_to_all x1, starting transfers between devices, body(): lax.all_to_all(send.reshape(nocc // oi, oi, oi * cm), 'occ', 0, 0)  27.5 us
    ppermute x9, waiting for transfers between devices, swap(): return lax.ppermute(x, 'vir', [(i, i ^ k) for i in range(nvirdev)])  20.6 us
    pallas_call x1, Pallas kernels, body(): pl.pallas_call(functools.partial(panel_kernel, steps), grid=(steps,), out...  6.99 us
    unnamed x16, local copies, waits for them, and re-layouts  6.06 us
    pallas_call x4, Pallas kernels, call(): pl.pallas_call(kernel, out_shape=outs, in_specs=specs, out_specs=whole(le...  5.2 us
    all_to_all x1, waiting for transfers between devices, body(): lax.all_to_all(send.reshape(nocc // oi, oi, oi * cm), 'occ', 0, 0)  3.36 us
  transfers between devices with their start and end apart: 10, of which 3 were waited for; matrix products, arithmetic and copies ran while one was open for 0% of the time, Pallas kernels for 7%

profile of v1, /device:TPU:8, one launch (start us, length us, event | category | flops | bytes accessed | tf_op | source)
XLA Modules:
  0.0 99.1 jit_solution(11072035934398750785)
XLA Ops:
  0.0 0.0 copy-start.1
  0.0 1.2 %copy-done.1 = f32[1024,256]{1,0:T(8,128)S(1)} copy-done((f32[1024,256]{1,0:T(8,128)S(1)}, f32[1024,256]{1,0:T(8,128)}, u32[]{:S(2)}) %copy-start.1) | copy-done | bytes 1048600
  1.2 0.0 copy-start.2
  1.2 0.7 copy-done.2
  1.9 0.0 copy-start.4
  1.9 0.7 copy-done.4
  2.6 0.0 copy-start.5
  2.6 0.7 copy-done.5
  3.2 2.2 %shard_map.55 = (f32[256,128]{1,0:T(8,128)S(1)}, f32[256,128]{1,0:T(8,128)}) custom-call(f32[1024,256]{1,0:T(8,128)S(1)} %copy-done.1, s32[1,256]{1,0:T(1,128)S(1)} %bitcast.5, s32[1,64]{1,0:T(1,128)S(1)} %bitcast.8, s32[1,2]{1,0:T(1,128)S(1)} %copy-done.4), custom_call_target="tpu_custom_call" | custom-call | flops 1000000000 | bytes 1312008 | tf_op jit(solution)/shard_map/pallas_call | solution.py:227
  5.4 27.5 %all-to-all-start = ((f32[64,4,128]{2,1,0:T(4,128)}), f32[64,4,128]{2,1,0:T(4,128)S(1)}, u32[]{:S(2)}, u32[]{:S(2)}) async-start(f32[64,4,128]{2,1,0:T(4,128)} %bitcast.2), calls=%async_computation | async-start | bytes 262144 | tf_op jit(solution)/shard_map/all_to_all | solution.py:256
  32.9 0.0 copy-start
  32.9 2.2 %copy-done = f32[256,4096]{1,0:T(8,128)S(1)} copy-done((f32[256,4096]{1,0:T(8,128)S(1)}, f32[256,4096]{1,0:T(8,128)}, u32[]{:S(2)}) %copy-start) | copy-done | bytes 4194328
  35.1 0.0 copy-start.6
  35.1 0.7 copy-done.6
  35.7 0.0 copy-start.3
  35.7 7.0 %shard_map.57 = (f32[128,256]{1,0:T(8,128)S(1)}, f32[128,256]{1,0:T(8,128)S(1)}, f32[128,256]{1,0:T(8,128)S(1)}, f32[128,256]{1,0:T(8,128)S(1)}) custom-call(f32[256,4096]{1,0:T(8,128)S(1)} %copy-done, s32[1,64]{1,0:T(1,128)S(1)} %bitcast.9), custom_call_target="tpu_custom_call" | custom-call | flops 2147483648 | bytes 8388608 | tf_op jit(solution)/shard_map/pallas_call | solution.py:260
  42.8 0.0 copy-start.7
  42.8 1.9 %collective-permute-start.3 = (f32[128,256]{1,0:T(8,128)S(1)}, f32[128,256]{1,0:T(8,128)S(1)}, u32[]{:S(2)}, u32[]{:S(2)}) collective-permute-start(f32[128,256]{1,0:T(8,128)S(1)} %get-tuple-element.18), channel_id=1, source_target_pairs={{0,1},{1,0},{2,3},{3,2},{4,5},{5,4},{6,7},{7,6},{8,9},{9,8},{10,11... | collective-permute-start | bytes 393224 | tf_op jit(solution)/shard_map/ppermute | solution.py:253
  44.7 3.4 %collective-permute-start.4 = (f32[128,256]{1,0:T(8,128)S(1)}, f32[128,256]{1,0:T(8,128)S(1)}, u32[]{:S(2)}, u32[]{:S(2)}) collective-permute-start(f32[128,256]{1,0:T(8,128)S(1)} %get-tuple-element.19), channel_id=1, source_target_pairs={{0,2},{1,3},{2,0},{3,1},{4,6},{5,7},{6,4},{7,5},{8,10},{9,11},{10,... | collective-permute-start | bytes 393224 | tf_op jit(solution)/shard_map/ppermute | solution.py:253
  48.1 2.3 %collective-permute-start.5 = (f32[128,256]{1,0:T(8,128)S(1)}, f32[128,256]{1,0:T(8,128)S(1)}, u32[]{:S(2)}, u32[]{:S(2)}) collective-permute-start(f32[128,256]{1,0:T(8,128)S(1)} %get-tuple-element.20), channel_id=1, source_target_pairs={{0,3},{1,2},{2,1},{3,0},{4,7},{5,6},{6,5},{7,4},{8,11},{9,10},{10,... | collective-permute-start | bytes 393224 | tf_op jit(solution)/shard_map/ppermute | solution.py:253
  50.4 3.4 %all-to-all-done = f32[64,4,128]{2,1,0:T(4,128)S(1)} async-done(((f32[64,4,128]{2,1,0:T(4,128)}), f32[64,4,128]{2,1,0:T(4,128)S(1)}, u32[]{:S(2)}, u32[]{:S(2)}) %all-to-all-start) | async-done | bytes 131104 | tf_op jit(solution)/shard_map/all_to_all | solution.py:256
  53.7 0.1 shard_map.56.refs_0_
  53.8 1.9 %collective-permute-start.2 = (f32[128,256]{1,0:T(8,128)S(1)}, f32[128,256]{1,0:T(8,128)S(1)}, u32[]{:S(2)}, u32[]{:S(2)}) collective-permute-start(f32[128,256]{1,0:T(8,128)S(1)} %shard_map.56.refs_0_), channel_id=1, source_target_pairs={{0,3},{1,2},{2,1},{3,0},{4,7},{5,6},{6,5},{7,4},{8,11},{9,10},{10,... | collective-permute-start | bytes 393224 | tf_op jit(solution)/shard_map/ppermute | solution.py:253
  55.8 1.9 %collective-permute-start.1 = (f32[128,256]{1,0:T(8,128)S(1)}, f32[128,256]{1,0:T(8,128)S(1)}, u32[]{:S(2)}, u32[]{:S(2)}) collective-permute-start(f32[128,256]{1,0:T(8,128)S(1)} %shard_map.56.refs_0_), channel_id=1, source_target_pairs={{0,2},{1,3},{2,0},{3,1},{4,6},{5,7},{6,4},{7,5},{8,10},{9,11},{10,... | collective-permute-start | bytes 393224 | tf_op jit(solution)/shard_map/ppermute | solution.py:253
  57.7 0.0 collective-permute-done.3.refs_5_
  57.7 3.7 %collective-permute-start = (f32[128,256]{1,0:T(8,128)S(1)}, f32[128,256]{1,0:T(8,128)S(1)}, u32[]{:S(2)}, u32[]{:S(2)}) collective-permute-start(f32[128,256]{1,0:T(8,128)S(1)} %shard_map.56.refs_0_), channel_id=1, source_target_pairs={{0,1},{1,0},{2,3},{3,2},{4,5},{5,4},{6,7},{7,6},{8,9},{9,8},{10,11... | collective-permute-start | bytes 393224 | tf_op jit(solution)/shard_map/ppermute | solution.py:253
  61.5 0.0 collective-permute-done.4.refs_6_
  61.5 0.0 collective-permute-done.5.refs_7_
  61.5 0.0 collective-permute-done.2.refs_3_
  61.5 2.0 %collective-permute-done.1.refs_2_ = f32[128,256]{1,0:T(8,128)S(1)} collective-permute-done((f32[128,256]{1,0:T(8,128)S(1)}, f32[128,256]{1,0:T(8,128)S(1)}, u32[]{:S(2)}, u32[]{:S(2)}) %collective-permute-start.1) | collective-permute-done | bytes 131104 | tf_op jit(solution)/shard_map/ppermute | solution.py:253
  63.5 0.0 collective-permute-done.refs_1_
  63.5 0.0 copy-done.3
  63.5 1.2 %shard_map.58 = (f32[128,256]{1,0:T(8,128)S(1)}, f32[128,256]{1,0:T(8,128)S(1)}, f32[128,256]{1,0:T(8,128)S(1)}, f32[128,256]{1,0:T(8,128)S(1)}) custom-call(f32[128,256]{1,0:T(8,128)S(1)} %shard_map.56.refs_0_, f32[128,256]{1,0:T(8,128)S(1)} %collective-permute-done.refs_1_, f32[128,256]{1,0:T(8,128)S(1)} %collective-permute-done.1.refs_2_, ...), custom_call_target="tpu_custom_call" | custom-call | flops 2000000000 | bytes 1573888 | tf_op jit(solution)/shard_map/pallas_call | solution.py:227
  64.7 3.0 %collective-permute-start.6 = (f32[128,256]{1,0:T(8,128)S(1)}, f32[128,256]{1,0:T(8,128)S(1)}, u32[]{:S(2)}, u32[]{:S(2)}) collective-permute-start(f32[128,256]{1,0:T(8,128)S(1)} %get-tuple-element.22), channel_id=1, source_target_pairs={{0,4},{1,5},{2,6},{3,7},{4,0},{5,1},{6,2},{7,3},{8,12},{9,13},{10,... | collective-permute-start | bytes 393224 | tf_op jit(solution)/shard_map/ppermute | solution.py:253
  67.6 8.9 %collective-permute-start.7 = (f32[128,256]{1,0:T(8,128)S(1)}, f32[128,256]{1,0:T(8,128)S(1)}, u32[]{:S(2)}, u32[]{:S(2)}) collective-permute-start(f32[128,256]{1,0:T(8,128)S(1)} %get-tuple-element.23), channel_id=1, source_target_pairs={{0,8},{1,9},{2,10},{3,11},{4,12},{5,13},{6,14},{7,15},{8,0},{9,1},... | collective-permute-start | bytes 393224 | tf_op jit(solution)/shard_map/ppermute | solution.py:253
  76.5 2.2 %collective-permute-start.8 = (f32[128,256]{1,0:T(8,128)S(1)}, f32[128,256]{1,0:T(8,128)S(1)}, u32[]{:S(2)}, u32[]{:S(2)}) collective-permute-start(f32[128,256]{1,0:T(8,128)S(1)} %get-tuple-element.24), channel_id=1, source_target_pairs={{0,12},{1,13},{2,14},{3,15},{4,8},{5,9},{6,10},{7,11},{8,4},{9,5},... | collective-permute-start | bytes 393224 | tf_op jit(solution)/shard_map/ppermute | solution.py:253
  78.7 0.0 collective-permute-done.6.refs_1_
  78.7 18.6 %collective-permute-done.7.refs_2_ = f32[128,256]{1,0:T(8,128)S(1)} collective-permute-done((f32[128,256]{1,0:T(8,128)S(1)}, f32[128,256]{1,0:T(8,128)S(1)}, u32[]{:S(2)}, u32[]{:S(2)}) %collective-permute-start.7) | collective-permute-done | bytes 131104 | tf_op jit(solution)/shard_map/ppermute | solution.py:253
  97.4 0.0 collective-permute-done.8.refs_3_
  97.4 0.0 copy-done.7
  97.4 1.7 %shard_map.59 = f32[1024,256]{1,0:T(8,128)} custom-call(f32[128,256]{1,0:T(8,128)S(1)} %get-tuple-element.21.refs_0_, f32[128,256]{1,0:T(8,128)S(1)} %collective-permute-done.6.refs_1_, f32[128,256]{1,0:T(8,128)S(1)} %collective-permute-done.7.refs_2_, f32[128,256]{1,0:T(8,128)S(1)} %collective-permute-done.8.refs_3_, s32[1,256]{1,0:T(1,128)S(1)} %bitcast.7, ...), custom_call_target="tpu_custom_call" | custom-call | flops 1000000000 | bytes 1574144 | tf_op jit(solution)/shard_map/pallas_call | solution.py:227
Async XLA Ops:
  0.0 1.2 %copy-start.1 = (f32[1024,256]{1,0:T(8,128)S(1)}, f32[1024,256]{1,0:T(8,128)}, u32[]{:S(2)}) copy-start(f32[1024,256]{1,0:T(8,128)} %amp_ref.1) | copy-start | bytes 3145732
  1.2 0.7 copy-start.2
  1.9 0.7 copy-start.4
  2.6 0.7 copy-start.5
  5.4 48.3 %all-to-all-start = ((f32[64,4,128]{2,1,0:T(4,128)}), f32[64,4,128]{2,1,0:T(4,128)S(1)}, u32[]{:S(2)}, u32[]{:S(2)}) async-start(f32[64,4,128]{2,1,0:T(4,128)} %bitcast.2), calls=%async_computation | async-start | bytes 262144 | tf_op jit(solution)/shard_map/all_to_all | solution.py:256
  32.9 2.2 %copy-start = (f32[256,4096]{1,0:T(8,128)S(1)}, f32[256,4096]{1,0:T(8,128)}, u32[]{:S(2)}) copy-start(f32[256,4096]{1,0:T(8,128)} %int_ref.1) | copy-start | bytes 12582916
  35.1 0.7 copy-start.6
  35.7 27.7 %copy-start.3 = (s32[256]{0:T(256)S(1)}, s32[256]{0:T(256)}, u32[]{:S(2)}) copy-start(s32[256]{0:T(256)} %param.7) | copy-start | bytes 3076
  42.8 54.6 %copy-start.7 = (s32[64]{0:T(128)S(1)}, s32[64]{0:T(128)}, u32[]{:S(2)}) copy-start(s32[64]{0:T(128)} %param.8) | copy-start | bytes 772
  42.8 14.9 %collective-permute-start.3 = (f32[128,256]{1,0:T(8,128)S(1)}, f32[128,256]{1,0:T(8,128)S(1)}, u32[]{:S(2)}, u32[]{:S(2)}) collective-permute-start(f32[128,256]{1,0:T(8,128)S(1)} %get-tuple-element.18), channel_id=1, source_target_pairs={{0,1},{1,0},{2,3},{3,2},{4,5},{5,4},{6,7},{7,6},{8,9},{9,8},{10,11... | collective-permute-start | bytes 393224 | tf_op jit(solution)/shard_map/ppermute | solution.py:253
  44.7 16.8 %collective-permute-start.4 = (f32[128,256]{1,0:T(8,128)S(1)}, f32[128,256]{1,0:T(8,128)S(1)}, u32[]{:S(2)}, u32[]{:S(2)}) collective-permute-start(f32[128,256]{1,0:T(8,128)S(1)} %get-tuple-element.19), channel_id=1, source_target_pairs={{0,2},{1,3},{2,0},{3,1},{4,6},{5,7},{6,4},{7,5},{8,10},{9,11},{10,... | collective-permute-start | bytes 393224 | tf_op jit(solution)/shard_map/ppermute | solution.py:253
  48.1 13.4 %collective-permute-start.5 = (f32[128,256]{1,0:T(8,128)S(1)}, f32[128,256]{1,0:T(8,128)S(1)}, u32[]{:S(2)}, u32[]{:S(2)}) collective-permute-start(f32[128,256]{1,0:T(8,128)S(1)} %get-tuple-element.20), channel_id=1, source_target_pairs={{0,3},{1,2},{2,1},{3,0},{4,7},{5,6},{6,5},{7,4},{8,11},{9,10},{10,... | collective-permute-start | bytes 393224 | tf_op jit(solution)/shard_map/ppermute | solution.py:253
  53.8 7.6 %collective-permute-start.2 = (f32[128,256]{1,0:T(8,128)S(1)}, f32[128,256]{1,0:T(8,128)S(1)}, u32[]{:S(2)}, u32[]{:S(2)}) collective-permute-start(f32[128,256]{1,0:T(8,128)S(1)} %shard_map.56.refs_0_), channel_id=1, source_target_pairs={{0,3},{1,2},{2,1},{3,0},{4,7},{5,6},{6,5},{7,4},{8,11},{9,10},{10,... | collective-permute-start | bytes 393224 | tf_op jit(solution)/shard_map/ppermute | solution.py:253
  55.8 7.7 %collective-permute-start.1 = (f32[128,256]{1,0:T(8,128)S(1)}, f32[128,256]{1,0:T(8,128)S(1)}, u32[]{:S(2)}, u32[]{:S(2)}) collective-permute-start(f32[128,256]{1,0:T(8,128)S(1)} %shard_map.56.refs_0_), channel_id=1, source_target_pairs={{0,2},{1,3},{2,0},{3,1},{4,6},{5,7},{6,4},{7,5},{8,10},{9,11},{10,... | collective-permute-start | bytes 393224 | tf_op jit(solution)/shard_map/ppermute | solution.py:253
  57.7 5.8 %collective-permute-start = (f32[128,256]{1,0:T(8,128)S(1)}, f32[128,256]{1,0:T(8,128)S(1)}, u32[]{:S(2)}, u32[]{:S(2)}) collective-permute-start(f32[128,256]{1,0:T(8,128)S(1)} %shard_map.56.refs_0_), channel_id=1, source_target_pairs={{0,1},{1,0},{2,3},{3,2},{4,5},{5,4},{6,7},{7,6},{8,9},{9,8},{10,11... | collective-permute-start | bytes 393224 | tf_op jit(solution)/shard_map/ppermute | solution.py:253
  64.7 14.0 %collective-permute-start.6 = (f32[128,256]{1,0:T(8,128)S(1)}, f32[128,256]{1,0:T(8,128)S(1)}, u32[]{:S(2)}, u32[]{:S(2)}) collective-permute-start(f32[128,256]{1,0:T(8,128)S(1)} %get-tuple-element.22), channel_id=1, source_target_pairs={{0,4},{1,5},{2,6},{3,7},{4,0},{5,1},{6,2},{7,3},{8,12},{9,13},{10,... | collective-permute-start | bytes 393224 | tf_op jit(solution)/shard_map/ppermute | solution.py:253
  67.6 29.7 %collective-permute-start.7 = (f32[128,256]{1,0:T(8,128)S(1)}, f32[128,256]{1,0:T(8,128)S(1)}, u32[]{:S(2)}, u32[]{:S(2)}) collective-permute-start(f32[128,256]{1,0:T(8,128)S(1)} %get-tuple-element.23), channel_id=1, source_target_pairs={{0,8},{1,9},{2,10},{3,11},{4,12},{5,13},{6,14},{7,15},{8,0},{9,1},... | collective-permute-start | bytes 393224 | tf_op jit(solution)/shard_map/ppermute | solution.py:253
  76.5 20.9 %collective-permute-start.8 = (f32[128,256]{1,0:T(8,128)S(1)}, f32[128,256]{1,0:T(8,128)S(1)}, u32[]{:S(2)}, u32[]{:S(2)}) collective-permute-start(f32[128,256]{1,0:T(8,128)S(1)} %get-tuple-element.24), channel_id=1, source_target_pairs={{0,12},{1,13},{2,14},{3,15},{4,8},{5,9},{6,10},{7,11},{8,4},{9,5},... | collective-permute-start | bytes 393224 | tf_op jit(solution)/shard_map/ppermute | solution.py:253

commit v2 on v1

v2 whole, which is shorter than its diff:
```python
import functools

import jax
import jax.numpy as jnp
from jax import lax
from jax.experimental import pallas as pl
from jax.experimental.pallas import tpu as pltpu
from jax.sharding import PartitionSpec as P

F32, BF16, I32 = jnp.float32, jnp.bfloat16, jnp.int32
CLASSES = 8
RANKS = 8
PAIR = 2
CHUNK = 512
VMEM = 48 * 1024 * 1024


def iota(shape, dim):
    return lax.broadcasted_iota(I32, shape, dim)


def pieces(value, count):
    out = []
    for step in range(count):
        part = value.astype(BF16)
        out.append(part)
        if step + 1 < count:
            value = value - part.astype(F32)
    return out


def dot(a, b):
    return lax.dot_general(a, b, (((1,), (0,)), ((), ())), preferred_element_type=F32)


def dot_nt(a, b):
    return lax.dot_general(a, b, (((1,), (1,)), ((), ())), preferred_element_type=F32)


def to_column(row):
    n = row.shape[1]
    return jnp.sum(jnp.where(iota((n, n), 0) == iota((n, n), 1), row, 0.0), axis=1, keepdims=True)


def pick_lanes(column, index):
    shape = (column.shape[0], index.shape[1])
    return jnp.sum(jnp.where(iota(shape, 0) == index, column, 0.0), axis=0, keepdims=True)


def pick_rows(row, index):
    shape = (index.shape[0], row.shape[1])
    return jnp.sum(jnp.where(iota(shape, 1) == index, row, 0.0), axis=1, keepdims=True)


def orbitals(vir_ref):
    row = vir_ref[...].astype(F32)
    col = to_column(row)
    n = row.shape[1]
    below = jnp.logical_and(col == row, iota((n, n), 1) < iota((n, n), 0))
    rank = jnp.sum(jnp.where(below, 1.0, 0.0), axis=1, keepdims=True)
    return row, col, rank


def pair_lanes(col, first, nvir, width):
    lane = iota((1, width * nvir), 1)
    one = pick_lanes(col, first + lane // nvir).astype(I32)
    two = pick_lanes(col, lane % nvir).astype(I32)
    return jnp.bitwise_xor(one, two)


def amps_kernel(amp_hbm, occ_hbm, vir_hbm, tile_hbm, own_ref, send_ref, amp_ref, occ_ref, vir_ref, tile_ref, sems):
    nocc, nvir = occ_ref.shape[1], vir_ref.shape[1]
    width = amp_ref.shape[1] // nvir
    oi = amp_ref.shape[0] // nocc
    small = [
        pltpu.make_async_copy(a, b, sems.at[oi + k])
        for k, (a, b) in enumerate(((vir_hbm, vir_ref), (occ_hbm, occ_ref), (tile_hbm, tile_ref)))
    ]
    blocks = [
        pltpu.make_async_copy(amp_hbm.at[pl.ds(k * nocc, nocc)], amp_ref.at[pl.ds(k * nocc, nocc)], sems.at[k])
        for k in range(oi)
    ]
    for copy in small + blocks:
        copy.start()
    for copy in small:
        copy.wait()
    o, v = lax.axis_index("occ"), lax.axis_index("vir")
    _, vcol, rank = orbitals(vir_ref)
    occ = occ_ref[...].astype(F32)
    irr_j = to_column(occ).astype(I32)
    sym_cd = pair_lanes(vcol, v * width, nvir, width)
    lane = iota((1, width * nvir), 1)
    tiles = tile_ref.shape[1]
    tile = jnp.zeros_like(lane)
    for t in range(tiles):
        tile = jnp.where(lane // (width * nvir // tiles) == t, tile_ref[0, t], tile)
    sym_cd = jnp.where(tile == 1, sym_cd, -1)
    cdr, n = width * nvir, oi * width * RANKS
    rank_rows = jnp.concatenate([rank] * width, axis=0).astype(I32)
    col = iota((cdr, n), 1)
    squeeze = jnp.logical_and((col // RANKS) % width == iota((cdr, n), 0) // nvir, col % RANKS == rank_rows)
    squeeze = jnp.where(squeeze, 1.0, 0.0).astype(BF16)
    lanes = iota((nocc, n), 1) // (width * RANKS)
    own = jnp.zeros((nocc, n), F32)
    for ii in range(oi):
        irr_i = pick_rows(occ, jnp.full((1, 1), o * oi + ii, I32)).astype(I32)
        keep = jnp.bitwise_xor(irr_j, irr_i) == sym_cd
        blocks[ii].wait()
        block = jnp.where(keep, amp_ref[ii * nocc:(ii + 1) * nocc, :], 0.0)
        short = sum(dot(part, squeeze) for part in pieces(block, 3))
        own = jnp.where(lanes == ii, short, own)
    own_ref[...] = own
    devices = nocc // oi
    lanes = iota((devices, n), 1) // (width * RANKS)
    swapped = [jnp.zeros((devices, n), F32) for _ in range(oi)]
    for jj in range(oi):
        rows = own_ref[pl.ds(jj, devices, stride=oi), :]
        for ii in range(oi):
            shift = (jj - ii) % oi * (width * RANKS)
            moved = pltpu.roll(rows, shift, 1) if shift else rows
            swapped[ii] = jnp.where(lanes == jj, moved, swapped[ii])
    for ii in range(oi):
        send_ref[pl.ds(ii, devices, stride=oi), :] = swapped[ii]


def panel_kernel(int_hbm, vir_hbm, keep_ref, send_ref, int_ref, vir_ref, fold_ref, high_ref, low_ref, sems):
    nvir = vir_ref.shape[1]
    cdr = int_ref.shape[0]
    steps = int_ref.shape[1] // CHUNK
    width = cdr // nvir
    first = pltpu.make_async_copy(vir_hbm, vir_ref, sems.at[steps])
    first.start()
    copies = [
        pltpu.make_async_copy(int_hbm.at[:, pl.ds(q * CHUNK, CHUNK)], int_ref.at[:, pl.ds(q * CHUNK, CHUNK)], sems.at[q])
        for q in range(steps)
    ]
    for copy in copies:
        copy.start()
    v = lax.axis_index("vir")
    first.wait()
    vrow, vcol, rank = orbitals(vir_ref)
    row = iota((cdr, 1), 0)
    sym_rows = jnp.bitwise_xor(pick_rows(vrow, v * width + row // nvir).astype(I32), pick_rows(vrow, row % nvir).astype(I32))
    lane = iota((1, CHUNK), 1)
    b = lane % nvir
    sym_b, rank_b = pick_lanes(vcol, b).astype(I32), pick_lanes(rank, b).astype(I32)
    n = nvir * RANKS
    cm = width * RANKS
    col = iota((n, 1), 0)
    code = ((col // cm) % 4 // 2 * 4 + (col // cm) // 4 % 2 * 8 + (col // cm) % 2 + col // (n // PAIR) * 2) ^ v
    code = code * cm + col % cm
    for q in range(steps):
        a = q * (CHUNK // nvir) + lane // nvir
        sym_ab = jnp.bitwise_xor(pick_lanes(vcol, a).astype(I32), sym_b)
        sym_ab = jnp.where(a == b, -1, sym_ab)
        plus = a * RANKS + rank_b
        minus = b * RANKS + pick_lanes(rank, a).astype(I32)
        at = slice(q * CHUNK, (q + 1) * CHUNK)
        fold_ref[:, at] = jnp.where(code == plus, 1.0, jnp.where(code == minus, -1.0, 0.0)).astype(BF16)
        copies[q].wait()
        high, low = pieces(jnp.where(sym_rows == sym_ab, int_ref[:, at], 0.0), 2)
        high_ref[:, at] = high
        low_ref[:, at] = low
    total = dot_nt(fold_ref[...], high_ref[...]) + dot_nt(fold_ref[...], low_ref[...])
    k = CLASSES * cm
    new = iota((cdr, k), 1)
    rank_rows = jnp.concatenate([rank] * width, axis=0).astype(I32)
    order = jnp.logical_and(new // cm == sym_rows, (new // RANKS) % width == row // nvir)
    order = jnp.logical_and(order, new % RANKS == rank_rows)
    order = jnp.where(order, 1.0, 0.0).astype(BF16)
    placed = sum(dot(piece, order) for piece in pieces(total, 2))
    keep_ref[...] = placed[:n // PAIR, :]
    send_ref[...] = placed[n // PAIR:, :]


def antisym_kernel(own_ref, got_ref, out_ref):
    out_ref[...] = (own_ref[...] - got_ref[...]).T


def ladder_kernel(oi, one_ref, two_ref, keep_ref, got_ref, occ_ref, mine_ref, mate_ref):
    nocc = occ_ref.shape[1]
    o = lax.axis_index("occ")
    occ = occ_ref[...].astype(F32)
    cm = one_ref.shape[0] // oi
    stacked = []
    for ref in (keep_ref, got_ref):
        high, low = pieces(ref[...], 2)
        stacked.append((jnp.concatenate([high, low], axis=0), high))
    n = keep_ref.shape[0]
    for ii in range(oi):
        irr_i = pick_rows(occ, jnp.full((1, 1), o * oi + ii, I32)).astype(I32)
        sym = jnp.bitwise_xor(occ_ref[...], irr_i)
        total = jnp.zeros((n, nocc), F32)
        at = slice(ii * cm, (ii + 1) * cm)
        for ref, (both, high) in zip((one_ref, two_ref), stacked, strict=True):
            block = ref[at, :]
            spread = jnp.concatenate([jnp.where(sym == s, block, 0.0) for s in range(CLASSES)], axis=0)
            upper, lower = pieces(spread, 2)
            first = dot(both, upper)
            total = total + (first[:n, :] + (first[n:, :] + dot(high, lower)))
        for k in range(n // (2 * cm)):
            mine_ref[k, at, :] = total[2 * k * cm:(2 * k + 1) * cm, :]
            mate_ref[k, at, :] = total[(2 * k + 1) * cm:(2 * k + 2) * cm, :]


def join_kernel(mine_ref, mate_ref, *outs):
    for k, out in enumerate(outs):
        out[...] = mine_ref[k] + mate_ref[k]


def far_kernel(far_ref, got_ref, out_ref):
    out_ref[...] = far_ref[...] + got_ref[...]


def spread_kernel(oi, own_ref, near_ref, far_ref, occ_ref, vir_ref, out_ref):
    nocc, nvir = occ_ref.shape[1], vir_ref.shape[1]
    width = out_ref.shape[1] // nvir
    o, v = lax.axis_index("occ"), lax.axis_index("vir")
    _, vcol, rank = orbitals(vir_ref)
    occ = occ_ref[...].astype(F32)
    irr_j = to_column(occ).astype(I32)
    sym_ab = pair_lanes(vcol, v * width, nvir, width)
    total = (own_ref[...] + near_ref[...] + far_ref[...]).T
    split = pieces(total, 3)
    n = total.shape[1]
    lane = iota((1, width * nvir), 1)
    rank_lanes = pick_lanes(rank, lane % nvir).astype(I32)
    row = iota((n, width * nvir), 0)
    open_ = jnp.logical_and((row // RANKS) % width == lane // nvir, row % RANKS == rank_lanes)
    for ii in range(oi):
        wide = jnp.where(jnp.logical_and(open_, row // (width * RANKS) == ii), 1.0, 0.0).astype(BF16)
        full = sum(dot(part, wide) for part in split)
        irr_i = pick_rows(occ, jnp.full((1, 1), o * oi + ii, I32)).astype(I32)
        keep = jnp.bitwise_xor(irr_j, irr_i) == sym_ab
        out_ref[ii * nocc:(ii + 1) * nocc, :] = jnp.where(keep, full, 0.0)


def spec(space):
    return pl.BlockSpec(memory_space=space)


def call(kernel, outs, ins, flops, interpret, space=pltpu.VMEM, scratch=()):
    moved = sum(x.size * 4 for x in ins) + sum(x.size * 4 for x in outs)
    return pl.pallas_call(
        kernel,
        out_shape=outs,
        in_specs=[spec(space)] * len(ins),
        out_specs=[spec(pltpu.VMEM)] * len(outs),
        scratch_shapes=scratch,
        compiler_params=pltpu.CompilerParams(vmem_limit_bytes=VMEM),
        cost_estimate=pl.CostEstimate(flops=flops, bytes_accessed=moved, transcendentals=0),
        interpret=interpret,
    )(*ins)


def pinned(x):
    return pltpu.with_memory_space_constraint(x, pltpu.HBM)


def array(*shape):
    return jax.ShapeDtypeStruct(shape, F32)


def body(nvirdev, interpret, amplitudes, integrals, occ_irrep, vir_irrep, tile_map):
    nocc, nvir = occ_irrep.shape[0], vir_irrep.shape[0]
    oi = amplitudes.shape[0] // nocc
    cdr = amplitudes.shape[1]
    width = cdr // nvir
    cm = width * RANKS
    n = nvir * RANKS
    occ = occ_irrep.reshape(1, nocc)
    vir = vir_irrep.reshape(1, nvir)

    def swap(x, k):
        return lax.ppermute(x, "vir", [(i, i ^ k) for i in range(nvirdev)])

    scratch = [
        pltpu.VMEM(amplitudes.shape, F32),
        pltpu.VMEM((1, nocc), I32),
        pltpu.VMEM((1, nvir), I32),
        pltpu.SMEM(tile_map.shape, I32),
        pltpu.SemaphoreType.DMA((oi + 3,)),
    ]
    ins = [pinned(x) for x in (amplitudes, occ, vir, tile_map)]
    own, send = call(amps_kernel, [array(nocc, oi * cm)] * 2, ins, 10**9, interpret, pltpu.HBM, scratch)
    got = lax.all_to_all(send.reshape(nocc // oi, oi, oi * cm), "occ", 0, 0).reshape(nocc, oi * cm)

    scratch = [
        pltpu.VMEM(integrals.shape, F32),
        pltpu.VMEM((1, nvir), I32),
        pltpu.VMEM((n, integrals.shape[1]), BF16),
        pltpu.VMEM(integrals.shape, BF16),
        pltpu.VMEM(integrals.shape, BF16),
        pltpu.SemaphoreType.DMA((integrals.shape[1] // CHUNK + 1,)),
    ]
    outs = [array(n // PAIR, CLASSES * cm)] * 2
    keep, give = call(panel_kernel, outs, [pinned(integrals), pinned(vir)], 4 * 10**9, interpret, pltpu.HBM, scratch)
    given = swap(give, 2)

    one = array(oi * cm, nocc)
    (anti,) = call(antisym_kernel, [one], [own, got], 10**6, interpret)
    far = nvirdev // 4
    mine, mate = call(
        functools.partial(ladder_kernel, oi),
        [array(far, oi * cm, nocc)] * 2,
        [anti, swap(anti, 2), keep, given, occ],
        2 * 10**9,
        interpret,
    )
    sums = call(join_kernel, [one] * far, [mine, swap(mate, 1)], 10**6, interpret)
    (far,) = call(far_kernel, [one], [sums[2], swap(sums[3], 4)], 10**6, interpret)
    far, near = swap(far, 8), swap(sums[1], 4)
    (out,) = call(
        functools.partial(spread_kernel, oi), [array(*amplitudes.shape)], [sums[0], near, far, occ, vir], 10**9, interpret
    )
    return out


def solution(mesh, interpret=False):
    placed = (P("occ", "vir"), P("vir", None), P(), P(), P("occ", "vir"))
    return jax.shard_map(
        functools.partial(body, mesh.shape["vir"], interpret),
        mesh=mesh,
        in_specs=placed,
        out_specs=P("occ", "vir"),
        check_vma=False,
    )
```

time: 99.6 us -> 99.4 us (level)
  the two profiles are of different devices: /device:TPU:8 before, /device:TPU:1 now
where the time goes in v2:
time: 99.4 us; the launch traced here: 99.1 us
  starting transfers between devices  53.1 us (53%)
  waiting for transfers between devices  33.6 us (34%)
  Pallas kernels  12.2 us (12%)
    all_to_all x1, starting transfers between devices, body(): lax.all_to_all(send.reshape(nocc // oi, oi, oi * cm), 'occ', 0, 0)  28 us
    ppermute x6, starting transfers between devices, swap(): return lax.ppermute(x, 'vir', [(i, i ^ k) for i in range(nvirdev)])  25.1 us
    ppermute x6, waiting for transfers between devices, swap(): return lax.ppermute(x, 'vir', [(i, i ^ k) for i in range(nvirdev)])  23.8 us
    pallas_call x7, Pallas kernels, call(): pl.pallas_call(kernel, out_shape=outs, in_specs=[spec(space)] * len(ins),...  12.2 us
    all_to_all x1, waiting for transfers between devices, body(): lax.all_to_all(send.reshape(nocc // oi, oi, oi * cm), 'occ', 0, 0)  9.84 us
  transfers between devices with their start and end apart: 7, of which 5 were waited for; matrix products, arithmetic and copies ran while one was open for 0% of the time, Pallas kernels for 6%

profile of v2, /device:TPU:1, one launch (start us, length us, event | category | flops | bytes accessed | tf_op | source)
XLA Modules:
  0.0 99.1 jit_solution(1844767745611779697)
XLA Ops:
  0.0 3.1 %shard_map.55 = (f32[256,128]{1,0:T(8,128)S(1)}, f32[256,128]{1,0:T(8,128)}) custom-call(f32[1024,256]{1,0:T(8,128)} %amp_hbm.1, s32[1,256]{1,0:T(1,128)} %bitcast.5, s32[1,64]{1,0:T(1,128)} %bitcast.8, s32[1,2]{1,0:T(1,128)} %tile_hbm.1), custom_call_target="tpu_custom_call" | custom-call | flops 1000000000 | bytes 1312008 | tf_op jit(solution)/shard_map/pallas_call | solution.py:244
  3.1 28.0 %all-to-all-start = ((f32[64,4,128]{2,1,0:T(4,128)}), f32[64,4,128]{2,1,0:T(4,128)S(1)}, u32[]{:S(2)}, u32[]{:S(2)}) async-start(f32[64,4,128]{2,1,0:T(4,128)} %bitcast.2), calls=%async_computation | async-start | bytes 262144 | tf_op jit(solution)/shard_map/all_to_all | solution.py:286
  31.1 0.0 copy-start
  31.1 6.1 %shard_map.57 = (f32[256,256]{1,0:T(8,128)S(1)}, f32[256,256]{1,0:T(8,128)S(1)}) custom-call(f32[256,4096]{1,0:T(8,128)} %int_hbm.1, s32[1,64]{1,0:T(1,128)} %bitcast.9), custom_call_target="tpu_custom_call" | custom-call | flops 4000000000 | bytes 4718848 | tf_op jit(solution)/shard_map/pallas_call | solution.py:244
  37.3 3.1 %collective-permute-start.1 = (f32[256,256]{1,0:T(8,128)S(1)}, f32[256,256]{1,0:T(8,128)S(1)}, u32[]{:S(2)}, u32[]{:S(2)}) collective-permute-start(f32[256,256]{1,0:T(8,128)S(1)} %get-tuple-element.18), channel_id=1, source_target_pairs={{0,2},{1,3},{2,0},{3,1},{4,6},{5,7},{6,4},{7,5},{8,10},{9,11},{10,... | collective-permute-start | bytes 786440 | tf_op jit(solution)/shard_map/ppermute | solution.py:275
  40.4 9.8 %all-to-all-done = f32[64,4,128]{2,1,0:T(4,128)S(1)} async-done(((f32[64,4,128]{2,1,0:T(4,128)}), f32[64,4,128]{2,1,0:T(4,128)S(1)}, u32[]{:S(2)}, u32[]{:S(2)}) %all-to-all-start) | async-done | bytes 131104 | tf_op jit(solution)/shard_map/all_to_all | solution.py:286
  50.2 0.1 shard_map.56.one_ref
  50.3 2.3 %collective-permute-start = (f32[128,256]{1,0:T(8,128)S(1)}, f32[128,256]{1,0:T(8,128)S(1)}, u32[]{:S(2)}, u32[]{:S(2)}) collective-permute-start(f32[128,256]{1,0:T(8,128)S(1)} %shard_map.56.one_ref), channel_id=1, source_target_pairs={{0,2},{1,3},{2,0},{3,1},{4,6},{5,7},{6,4},{7,5},{8,10},{9,11},{10,... | collective-permute-start | bytes 393224 | tf_op jit(solution)/shard_map/ppermute | solution.py:275
  52.7 0.0 collective-permute-done.1.got_ref
  52.7 3.4 %collective-permute-done.two_ref = f32[128,256]{1,0:T(8,128)S(1)} collective-permute-done((f32[128,256]{1,0:T(8,128)S(1)}, f32[128,256]{1,0:T(8,128)S(1)}, u32[]{:S(2)}, u32[]{:S(2)}) %collective-permute-start) | collective-permute-done | bytes 131104 | tf_op jit(solution)/shard_map/ppermute | solution.py:275
  56.0 0.0 copy-done
  56.0 0.0 copy-start.1
  56.0 1.1 %shard_map.58 = (f32[4,128,256]{2,1,0:T(8,128)S(1)}, f32[4,128,256]{2,1,0:T(8,128)S(1)}) custom-call(f32[128,256]{1,0:T(8,128)S(1)} %shard_map.56.one_ref, f32[128,256]{1,0:T(8,128)S(1)} %collective-permute-done.two_ref, f32[256,256]{1,0:T(8,128)S(1)} %get-tuple-element.17.keep_ref, f32[256,256]{1,0:T(8,128)S(1)} %collective-permute-done.1.got_ref, ...), custom_call_target="tpu_custom_call" | custom-call | flops 2000000000 | bytes 1836032 | tf_op jit(solution)/shard_map/pallas_call | solution.py:244
  57.2 6.7 %collective-permute-start.2 = (f32[4,128,256]{2,1,0:T(8,128)S(1)}, f32[4,128,256]{2,1,0:T(8,128)S(1)}, u32[]{:S(2)}, u32[]{:S(2)}) collective-permute-start(f32[4,128,256]{2,1,0:T(8,128)S(1)} %get-tuple-element.20), channel_id=1, source_target_pairs={{0,1},{1,0},{2,3},{3,2},{4,5},{5,4},{6,7},{7,6},{8,9},{9,8},{10,11... | collective-permute-start | bytes 1572872 | tf_op jit(solution)/shard_map/ppermute | solution.py:275
  63.8 1.5 %collective-permute-done.2.mate_ref = f32[4,128,256]{2,1,0:T(8,128)S(1)} collective-permute-done((f32[4,128,256]{2,1,0:T(8,128)S(1)}, f32[4,128,256]{2,1,0:T(8,128)S(1)}, u32[]{:S(2)}, u32[]{:S(2)}) %collective-permute-start.2) | collective-permute-done | bytes 524320 | tf_op jit(solution)/shard_map/ppermute | solution.py:275
  65.4 0.1 shard_map.59
  65.4 2.3 %collective-permute-start.4 = (f32[128,256]{1,0:T(8,128)S(1)}, f32[128,256]{1,0:T(8,128)S(1)}, u32[]{:S(2)}, u32[]{:S(2)}) collective-permute-start(f32[128,256]{1,0:T(8,128)S(1)} %get-tuple-element.24), channel_id=1, source_target_pairs={{0,4},{1,5},{2,6},{3,7},{4,0},{5,1},{6,2},{7,3},{8,12},{9,13},{10,... | collective-permute-start | bytes 393224 | tf_op jit(solution)/shard_map/ppermute | solution.py:275
  67.8 3.8 %collective-permute-start.3 = (f32[128,256]{1,0:T(8,128)S(1)}, f32[128,256]{1,0:T(8,128)S(1)}, u32[]{:S(2)}, u32[]{:S(2)}) collective-permute-start(f32[128,256]{1,0:T(8,128)S(1)} %get-tuple-element.22), channel_id=1, source_target_pairs={{0,4},{1,5},{2,6},{3,7},{4,0},{5,1},{6,2},{7,3},{8,12},{9,13},{10,... | collective-permute-start | bytes 393224 | tf_op jit(solution)/shard_map/ppermute | solution.py:275
  71.6 7.1 %collective-permute-done.4.got_ref = f32[128,256]{1,0:T(8,128)S(1)} collective-permute-done((f32[128,256]{1,0:T(8,128)S(1)}, f32[128,256]{1,0:T(8,128)S(1)}, u32[]{:S(2)}, u32[]{:S(2)}) %collective-permute-start.4) | collective-permute-done | bytes 131104 | tf_op jit(solution)/shard_map/ppermute | solution.py:275
  78.7 6.8 %collective-permute-start.5 = (f32[128,256]{1,0:T(8,128)S(1)}, f32[128,256]{1,0:T(8,128)S(1)}, u32[]{:S(2)}, u32[]{:S(2)}) collective-permute-start(f32[128,256]{1,0:T(8,128)S(1)} %shard_map.60), channel_id=1, source_target_pairs={{0,8},{1,9},{2,10},{3,11},{4,12},{5,13},{6,14},{7,15},{8,0},{9,1},... | collective-permute-start | bytes 393224 | tf_op jit(solution)/shard_map/ppermute | solution.py:275
  85.6 0.0 collective-permute-done.3.near_ref
  85.6 11.8 %collective-permute-done.5.far_ref = f32[128,256]{1,0:T(8,128)S(1)} collective-permute-done((f32[128,256]{1,0:T(8,128)S(1)}, f32[128,256]{1,0:T(8,128)S(1)}, u32[]{:S(2)}, u32[]{:S(2)}) %collective-permute-start.5) | collective-permute-done | bytes 131104 | tf_op jit(solution)/shard_map/ppermute | solution.py:275
  97.4 0.0 copy-done.1
  97.4 1.7 %shard_map.61 = f32[1024,256]{1,0:T(8,128)} custom-call(f32[128,256]{1,0:T(8,128)S(1)} %get-tuple-element.21.own_ref, f32[128,256]{1,0:T(8,128)S(1)} %collective-permute-done.3.near_ref, f32[128,256]{1,0:T(8,128)S(1)} %collective-permute-done.5.far_ref, s32[1,256]{1,0:T(1,128)S(1)} %bitcast.7, s32[1,64]{1,0:T(1,128)S(1)} %bitcast.10), custom_call_target="tpu_custom_call" | custom-call | flops 1000000000 | bytes 1443072 | tf_op jit(solution)/shard_map/pallas_call | solution.py:244
  (1 shorter events, 0.0 us)
Async XLA Ops:
  3.1 47.1 %all-to-all-start = ((f32[64,4,128]{2,1,0:T(4,128)}), f32[64,4,128]{2,1,0:T(4,128)S(1)}, u32[]{:S(2)}, u32[]{:S(2)}) async-start(f32[64,4,128]{2,1,0:T(4,128)} %bitcast.2), calls=%async_computation | async-start | bytes 262144 | tf_op jit(solution)/shard_map/all_to_all | solution.py:286
  31.1 24.9 %copy-start = (s32[256]{0:T(256)S(1)}, s32[256]{0:T(256)}, u32[]{:S(2)}) copy-start(s32[256]{0:T(256)} %param.7) | copy-start | bytes 3076
  37.3 15.4 %collective-permute-start.1 = (f32[256,256]{1,0:T(8,128)S(1)}, f32[256,256]{1,0:T(8,128)S(1)}, u32[]{:S(2)}, u32[]{:S(2)}) collective-permute-start(f32[256,256]{1,0:T(8,128)S(1)} %get-tuple-element.18), channel_id=1, source_target_pairs={{0,2},{1,3},{2,0},{3,1},{4,6},{5,7},{6,4},{7,5},{8,10},{9,11},{10,... | collective-permute-start | bytes 786440 | tf_op jit(solution)/shard_map/ppermute | solution.py:275
  50.3 5.7 %collective-permute-start = (f32[128,256]{1,0:T(8,128)S(1)}, f32[128,256]{1,0:T(8,128)S(1)}, u32[]{:S(2)}, u32[]{:S(2)}) collective-permute-start(f32[128,256]{1,0:T(8,128)S(1)} %shard_map.56.one_ref), channel_id=1, source_target_pairs={{0,2},{1,3},{2,0},{3,1},{4,6},{5,7},{6,4},{7,5},{8,10},{9,11},{10,... | collective-permute-start | bytes 393224 | tf_op jit(solution)/shard_map/ppermute | solution.py:275
  56.0 41.3 %copy-start.1 = (s32[64]{0:T(128)S(1)}, s32[64]{0:T(128)}, u32[]{:S(2)}) copy-start(s32[64]{0:T(128)} %param.8) | copy-start | bytes 772
  57.2 8.2 %collective-permute-start.2 = (f32[4,128,256]{2,1,0:T(8,128)S(1)}, f32[4,128,256]{2,1,0:T(8,128)S(1)}, u32[]{:S(2)}, u32[]{:S(2)}) collective-permute-start(f32[4,128,256]{2,1,0:T(8,128)S(1)} %get-tuple-element.20), channel_id=1, source_target_pairs={{0,1},{1,0},{2,3},{3,2},{4,5},{5,4},{6,7},{7,6},{8,9},{9,8},{10,11... | collective-permute-start | bytes 1572872 | tf_op jit(solution)/shard_map/ppermute | solution.py:275
  65.4 13.3 %collective-permute-start.4 = (f32[128,256]{1,0:T(8,128)S(1)}, f32[128,256]{1,0:T(8,128)S(1)}, u32[]{:S(2)}, u32[]{:S(2)}) collective-permute-start(f32[128,256]{1,0:T(8,128)S(1)} %get-tuple-element.24), channel_id=1, source_target_pairs={{0,4},{1,5},{2,6},{3,7},{4,0},{5,1},{6,2},{7,3},{8,12},{9,13},{10,... | collective-permute-start | bytes 393224 | tf_op jit(solution)/shard_map/ppermute | solution.py:275
  67.8 17.8 %collective-permute-start.3 = (f32[128,256]{1,0:T(8,128)S(1)}, f32[128,256]{1,0:T(8,128)S(1)}, u32[]{:S(2)}, u32[]{:S(2)}) collective-permute-start(f32[128,256]{1,0:T(8,128)S(1)} %get-tuple-element.22), channel_id=1, source_target_pairs={{0,4},{1,5},{2,6},{3,7},{4,0},{5,1},{6,2},{7,3},{8,12},{9,13},{10,... | collective-permute-start | bytes 393224 | tf_op jit(solution)/shard_map/ppermute | solution.py:275
  78.7 18.6 %collective-permute-start.5 = (f32[128,256]{1,0:T(8,128)S(1)}, f32[128,256]{1,0:T(8,128)S(1)}, u32[]{:S(2)}, u32[]{:S(2)}) collective-permute-start(f32[128,256]{1,0:T(8,128)S(1)} %shard_map.60), channel_id=1, source_target_pairs={{0,8},{1,9},{2,10},{3,11},{4,12},{5,13},{6,14},{7,15},{8,0},{9,1},... | collective-permute-start | bytes 393224 | tf_op jit(solution)/shard_map/ppermute | solution.py:275

commit v3 on v2

--- a/solution.py
+++ b/solution.py
@@ -68,7 +68,7 @@
     return jnp.bitwise_xor(one, two)
 
 
-def amps_kernel(amp_hbm, occ_hbm, vir_hbm, tile_hbm, own_ref, send_ref, amp_ref, occ_ref, vir_ref, tile_ref, sems):
+def amps_kernel(amp_hbm, occ_hbm, vir_hbm, tile_hbm, own_ref, stay_ref, hop_ref, amp_ref, occ_ref, vir_ref, tile_ref, send_ref, sems):
     nocc, nvir = occ_ref.shape[1], vir_ref.shape[1]
     width = amp_ref.shape[1] // nvir
     oi = amp_ref.shape[0] // nocc
@@ -121,6 +121,10 @@
             swapped[ii] = jnp.where(lanes == jj, moved, swapped[ii])
     for ii in range(oi):
         send_ref[pl.ds(ii, devices, stride=oi), :] = swapped[ii]
+    rows = nocc // 2
+    high = o // (devices // 2)
+    stay_ref[...] = jnp.where(high == 0, send_ref[:rows, :], send_ref[rows:, :])
+    hop_ref[...] = jnp.where(high == 0, send_ref[rows:, :], send_ref[:rows, :])
 
 
 def panel_kernel(int_hbm, vir_hbm, keep_ref, send_ref, int_ref, vir_ref, fold_ref, high_ref, low_ref, sems):
@@ -173,8 +177,24 @@
     send_ref[...] = placed[n // PAIR:, :]
 
 
-def antisym_kernel(own_ref, got_ref, out_ref):
-    out_ref[...] = (own_ref[...] - got_ref[...]).T
+def merge_kernel(oi, stay_ref, hop_ref, out_ref):
+    half = stay_ref.shape[0] // oi
+    for k, ref in enumerate((stay_ref, hop_ref)):
+        for b in range(oi):
+            out_ref[pl.ds(k * oi + b, half, stride=2 * oi), :] = ref[pl.ds(b, half, stride=oi), :]
+
+
+def antisym_kernel(oi, own_ref, got_ref, out_ref, diff_ref):
+    rows = own_ref.shape[0] // 2
+    half = rows // oi
+    high = lax.axis_index("occ") // half
+    for b in range(oi):
+        same = got_ref[pl.ds(b, half, stride=2 * oi), :]
+        other = got_ref[pl.ds(oi + b, half, stride=2 * oi), :]
+        for h in range(2):
+            at = pl.ds(h * rows + b, half, stride=oi)
+            diff_ref[at, :] = own_ref[at, :] - jnp.where(high == h, same, other)
+    out_ref[...] = diff_ref[...].T
 
 
 def ladder_kernel(oi, one_ref, two_ref, keep_ref, got_ref, occ_ref, mine_ref, mate_ref):
@@ -279,12 +299,14 @@
         pltpu.VMEM((1, nocc), I32),
         pltpu.VMEM((1, nvir), I32),
         pltpu.SMEM(tile_map.shape, I32),
+        pltpu.VMEM((nocc, oi * cm), F32),
         pltpu.SemaphoreType.DMA((oi + 3,)),
     ]
     ins = [pinned(x) for x in (amplitudes, occ, vir, tile_map)]
-    own, send = call(amps_kernel, [array(nocc, oi * cm)] * 2, ins, 10**9, interpret, pltpu.HBM, scratch)
-    got = lax.all_to_all(send.reshape(nocc // oi, oi, oi * cm), "occ", 0, 0).reshape(nocc, oi * cm)
-
+    half = array(nocc // 2, oi * cm)
+    own, stay, hop = call(amps_kernel, [array(nocc, oi * cm), half, half], ins, 10**9, interpret, pltpu.HBM, scratch)
+    devices = nocc // oi
+    hop = lax.ppermute(hop, "occ", [(i, (i + devices // 2) % devices) for i in range(devices)])
     scratch = [
         pltpu.VMEM(integrals.shape, F32),
         pltpu.VMEM((1, nvir), I32),
@@ -295,10 +317,18 @@
     ]
     outs = [array(n // PAIR, CLASSES * cm)] * 2
     keep, give = call(panel_kernel, outs, [pinned(integrals), pinned(vir)], 4 * 10**9, interpret, pltpu.HBM, scratch)
+    stay, keep = lax.optimization_barrier((stay, keep))
     given = swap(give, 2)
 
+    (send,) = call(functools.partial(merge_kernel, oi), [array(nocc, oi * cm)], [stay, hop], 10**6, interpret)
+    halves = [list(range(devices // 2)), list(range(devices // 2, devices))]
+    got = lax.all_to_all(send.reshape(devices // 2, 2 * oi, oi * cm), "occ", 0, 0, axis_index_groups=halves)
+    got = got.reshape(nocc, oi * cm)
+
+
     one = array(oi * cm, nocc)
-    (anti,) = call(antisym_kernel, [one], [own, got], 10**6, interpret)
+    scratch = [pltpu.VMEM((nocc, oi * cm), F32)]
+    (anti,) = call(functools.partial(antisym_kernel, oi), [one], [own, got], 10**6, interpret, scratch=scratch)
     far = nvirdev // 4
     mine, mate = call(
         functools.partial(ladder_kernel, oi),

time: 99.4 us -> 94.1 us (0.947)
  the two profiles are of different devices: /device:TPU:1 before, /device:TPU:8 now
where the time goes in v3:
time: 94.1 us; the launch traced here: 93.7 us
  starting transfers between devices  51 us (54%)
  waiting for transfers between devices  30.2 us (32%)
  Pallas kernels  12.3 us (13%)
    ppermute x6, waiting for transfers between devices, swap(): return lax.ppermute(x, 'vir', [(i, i ^ k) for i in range(nvirdev)])  24 us
    ppermute x6, starting transfers between devices, swap(): return lax.ppermute(x, 'vir', [(i, i ^ k) for i in range(nvirdev)])  21.5 us
    ppermute x1, starting transfers between devices, body(): lax.ppermute(hop, 'occ', [(i, (i + devices // 2) % devices) for i in rang...  19.4 us
    pallas_call x8, Pallas kernels, call(): pl.pallas_call(kernel, out_shape=outs, in_specs=[spec(space)] * len(ins),...  12.3 us
    all_to_all x1, starting transfers between devices, body(): lax.all_to_all(send.reshape(devices // 2, 2 * oi, oi * cm), 'occ', 0, 0,...  10.2 us
    all_to_all x1, waiting for transfers between devices, body(): lax.all_to_all(send.reshape(devices // 2, 2 * oi, oi * cm), 'occ', 0, 0,...  6.28 us
  transfers between devices with their start and end apart: 8, of which 5 were waited for; matrix products, arithmetic and copies ran while one was open for 0% of the time, Pallas kernels for 7%

profile of v3, /device:TPU:8, one launch (start us, length us, event | category | flops | bytes accessed | tf_op | source)
XLA Modules:
  0.0 93.7 jit_solution(17916376589905714096)
XLA Ops:
  0.0 2.4 %shard_map.55 = (f32[256,128]{1,0:T(8,128)S(1)}, f32[128,128]{1,0:T(8,128)S(1)}, f32[128,128]{1,0:T(8,128)S(1)}) custom-call(f32[1024,256]{1,0:T(8,128)} %amp_hbm.1, s32[1,256]{1,0:T(1,128)} %bitcast.5, s32[1,64]{1,0:T(1,128)} %bitcast.8, s32[1,2]{1,0:T(1,128)} %tile_hbm.1), custom_call_target="tpu_custom_call" | custom-call | flops 1000000000 | bytes 1312008 | tf_op jit(solution)/shard_map/pallas_call | solution.py:264
  2.4 0.0 copy-start
  2.5 19.4 %collective-permute-start = (f32[128,128]{1,0:T(8,128)S(1)}, f32[128,128]{1,0:T(8,128)S(1)}, u32[]{:S(2)}, u32[]{:S(2)}) collective-permute-start(f32[128,128]{1,0:T(8,128)S(1)} %get-tuple-element.22), channel_id=1, source_target_pairs={{0,512},{16,528},{32,544},{48,560},{64,576},{80,592},{96,608},{112... | collective-permute-start | bytes 196616 | tf_op jit(solution)/shard_map/ppermute | solution.py:309
  21.8 6.1 %shard_map.56 = (f32[256,256]{1,0:T(8,128)S(1)}, f32[256,256]{1,0:T(8,128)S(1)}) custom-call(f32[256,4096]{1,0:T(8,128)} %int_hbm.1, s32[1,64]{1,0:T(1,128)} %bitcast.9), custom_call_target="tpu_custom_call" | custom-call | flops 4000000000 | bytes 4718848 | tf_op jit(solution)/shard_map/pallas_call | solution.py:264
  28.0 0.0 collective-permute-done.hop_ref
  28.0 0.7 shard_map.57
  28.7 10.2 %all-to-all-start = ((f32[32,8,128]{2,1,0:T(8,128)}), f32[32,8,128]{2,1,0:T(8,128)S(1)}, u32[]{:S(2)}, u32[]{:S(2)}) async-start(f32[32,8,128]{2,1,0:T(8,128)} %bitcast.2), calls=%async_computation | async-start | bytes 262144 | tf_op jit(solution)/shard_map/all_to_all | solution.py:325
  38.8 3.4 %collective-permute-start.2 = (f32[256,256]{1,0:T(8,128)S(1)}, f32[256,256]{1,0:T(8,128)S(1)}, u32[]{:S(2)}, u32[]{:S(2)}) collective-permute-start(f32[256,256]{1,0:T(8,128)S(1)} %get-tuple-element.24), channel_id=1, source_target_pairs={{0,2},{1,3},{2,0},{3,1},{4,6},{5,7},{6,4},{7,5},{8,10},{9,11},{10,... | collective-permute-start | bytes 786440 | tf_op jit(solution)/shard_map/ppermute | solution.py:295
  42.2 6.3 %all-to-all-done = f32[32,8,128]{2,1,0:T(8,128)S(1)} async-done(((f32[32,8,128]{2,1,0:T(8,128)}), f32[32,8,128]{2,1,0:T(8,128)S(1)}, u32[]{:S(2)}, u32[]{:S(2)}) %all-to-all-start) | async-done | bytes 131104 | tf_op jit(solution)/shard_map/all_to_all | solution.py:325
  48.5 0.1 shard_map.58.one_ref
  48.6 0.0 copy-start.1
  48.6 3.4 %collective-permute-start.1 = (f32[128,256]{1,0:T(8,128)S(1)}, f32[128,256]{1,0:T(8,128)S(1)}, u32[]{:S(2)}, u32[]{:S(2)}) collective-permute-start(f32[128,256]{1,0:T(8,128)S(1)} %shard_map.58.one_ref), channel_id=1, source_target_pairs={{0,2},{1,3},{2,0},{3,1},{4,6},{5,7},{6,4},{7,5},{8,10},{9,11},{10,... | collective-permute-start | bytes 393224 | tf_op jit(solution)/shard_map/ppermute | solution.py:295
  52.0 0.0 collective-permute-done.2.got_ref
  52.0 3.5 %collective-permute-done.1.two_ref = f32[128,256]{1,0:T(8,128)S(1)} collective-permute-done((f32[128,256]{1,0:T(8,128)S(1)}, f32[128,256]{1,0:T(8,128)S(1)}, u32[]{:S(2)}, u32[]{:S(2)}) %collective-permute-start.1) | collective-permute-done | bytes 131104 | tf_op jit(solution)/shard_map/ppermute | solution.py:295
  55.5 0.0 copy-done
  55.5 1.1 %shard_map.59 = (f32[4,128,256]{2,1,0:T(8,128)S(1)}, f32[4,128,256]{2,1,0:T(8,128)S(1)}) custom-call(f32[128,256]{1,0:T(8,128)S(1)} %shard_map.58.one_ref, f32[128,256]{1,0:T(8,128)S(1)} %collective-permute-done.1.two_ref, f32[256,256]{1,0:T(8,128)S(1)} %get-tuple-element.23.keep_ref, f32[256,256]{1,0:T(8,128)S(1)} %collective-permute-done.2.got_ref, ...), custom_call_target="tpu_custom_call" | custom-call | flops 2000000000 | bytes 1836032 | tf_op jit(solution)/shard_map/pallas_call | solution.py:264
  56.6 1.9 %collective-permute-start.3 = (f32[4,128,256]{2,1,0:T(8,128)S(1)}, f32[4,128,256]{2,1,0:T(8,128)S(1)}, u32[]{:S(2)}, u32[]{:S(2)}) collective-permute-start(f32[4,128,256]{2,1,0:T(8,128)S(1)} %get-tuple-element.26), channel_id=1, source_target_pairs={{0,1},{1,0},{2,3},{3,2},{4,5},{5,4},{6,7},{7,6},{8,9},{9,8},{10,11... | collective-permute-start | bytes 1572872 | tf_op jit(solution)/shard_map/ppermute | solution.py:295
  58.6 1.9 %collective-permute-done.3.mate_ref = f32[4,128,256]{2,1,0:T(8,128)S(1)} collective-permute-done((f32[4,128,256]{2,1,0:T(8,128)S(1)}, f32[4,128,256]{2,1,0:T(8,128)S(1)}, u32[]{:S(2)}, u32[]{:S(2)}) %collective-permute-start.3) | collective-permute-done | bytes 524320 | tf_op jit(solution)/shard_map/ppermute | solution.py:295
  60.4 0.1 shard_map.60
  60.5 4.3 %collective-permute-start.5 = (f32[128,256]{1,0:T(8,128)S(1)}, f32[128,256]{1,0:T(8,128)S(1)}, u32[]{:S(2)}, u32[]{:S(2)}) collective-permute-start(f32[128,256]{1,0:T(8,128)S(1)} %get-tuple-element.30), channel_id=1, source_target_pairs={{0,4},{1,5},{2,6},{3,7},{4,0},{5,1},{6,2},{7,3},{8,12},{9,13},{10,... | collective-permute-start | bytes 393224 | tf_op jit(solution)/shard_map/ppermute | solution.py:295
  64.8 2.5 %collective-permute-start.4 = (f32[128,256]{1,0:T(8,128)S(1)}, f32[128,256]{1,0:T(8,128)S(1)}, u32[]{:S(2)}, u32[]{:S(2)}) collective-permute-start(f32[128,256]{1,0:T(8,128)S(1)} %get-tuple-element.28), channel_id=1, source_target_pairs={{0,4},{1,5},{2,6},{3,7},{4,0},{5,1},{6,2},{7,3},{8,12},{9,13},{10,... | collective-permute-start | bytes 393224 | tf_op jit(solution)/shard_map/ppermute | solution.py:295
  67.3 8.0 %collective-permute-done.5.got_ref = f32[128,256]{1,0:T(8,128)S(1)} collective-permute-done((f32[128,256]{1,0:T(8,128)S(1)}, f32[128,256]{1,0:T(8,128)S(1)}, u32[]{:S(2)}, u32[]{:S(2)}) %collective-permute-start.5) | collective-permute-done | bytes 131104 | tf_op jit(solution)/shard_map/ppermute | solution.py:295
  75.3 6.1 %collective-permute-start.6 = (f32[128,256]{1,0:T(8,128)S(1)}, f32[128,256]{1,0:T(8,128)S(1)}, u32[]{:S(2)}, u32[]{:S(2)}) collective-permute-start(f32[128,256]{1,0:T(8,128)S(1)} %shard_map.61), channel_id=1, source_target_pairs={{0,8},{1,9},{2,10},{3,11},{4,12},{5,13},{6,14},{7,15},{8,0},{9,1},... | collective-permute-start | bytes 393224 | tf_op jit(solution)/shard_map/ppermute | solution.py:295
  81.4 0.0 collective-permute-done.4.near_ref
  81.4 10.6 %collective-permute-done.6.far_ref = f32[128,256]{1,0:T(8,128)S(1)} collective-permute-done((f32[128,256]{1,0:T(8,128)S(1)}, f32[128,256]{1,0:T(8,128)S(1)}, u32[]{:S(2)}, u32[]{:S(2)}) %collective-permute-start.6) | collective-permute-done | bytes 131104 | tf_op jit(solution)/shard_map/ppermute | solution.py:295
  92.0 0.0 copy-done.1
  92.0 1.7 %shard_map.62 = f32[1024,256]{1,0:T(8,128)} custom-call(f32[128,256]{1,0:T(8,128)S(1)} %get-tuple-element.27.own_ref, f32[128,256]{1,0:T(8,128)S(1)} %collective-permute-done.4.near_ref, f32[128,256]{1,0:T(8,128)S(1)} %collective-permute-done.6.far_ref, s32[1,256]{1,0:T(1,128)S(1)} %bitcast.7, s32[1,64]{1,0:T(1,128)S(1)} %bitcast.10), custom_call_target="tpu_custom_call" | custom-call | flops 1000000000 | bytes 1443072 | tf_op jit(solution)/shard_map/pallas_call | solution.py:264
  (1 shorter events, 0.0 us)
Async XLA Ops:
  2.4 53.1 %copy-start = (s32[256]{0:T(256)S(1)}, s32[256]{0:T(256)}, u32[]{:S(2)}) copy-start(s32[256]{0:T(256)} %param.7) | copy-start | bytes 3076
  2.5 25.5 %collective-permute-start = (f32[128,128]{1,0:T(8,128)S(1)}, f32[128,128]{1,0:T(8,128)S(1)}, u32[]{:S(2)}, u32[]{:S(2)}) collective-permute-start(f32[128,128]{1,0:T(8,128)S(1)} %get-tuple-element.22), channel_id=1, source_target_pairs={{0,512},{16,528},{32,544},{48,560},{64,576},{80,592},{96,608},{112... | collective-permute-start | bytes 196616 | tf_op jit(solution)/shard_map/ppermute | solution.py:309
  28.7 19.8 %all-to-all-start = ((f32[32,8,128]{2,1,0:T(8,128)}), f32[32,8,128]{2,1,0:T(8,128)S(1)}, u32[]{:S(2)}, u32[]{:S(2)}) async-start(f32[32,8,128]{2,1,0:T(8,128)} %bitcast.2), calls=%async_computation | async-start | bytes 262144 | tf_op jit(solution)/shard_map/all_to_all | solution.py:325
  38.8 13.2 %collective-permute-start.2 = (f32[256,256]{1,0:T(8,128)S(1)}, f32[256,256]{1,0:T(8,128)S(1)}, u32[]{:S(2)}, u32[]{:S(2)}) collective-permute-start(f32[256,256]{1,0:T(8,128)S(1)} %get-tuple-element.24), channel_id=1, source_target_pairs={{0,2},{1,3},{2,0},{3,1},{4,6},{5,7},{6,4},{7,5},{8,10},{9,11},{10,... | collective-permute-start | bytes 786440 | tf_op jit(solution)/shard_map/ppermute | solution.py:295
  48.6 43.4 %copy-start.1 = (s32[64]{0:T(128)S(1)}, s32[64]{0:T(128)}, u32[]{:S(2)}) copy-start(s32[64]{0:T(128)} %param.8) | copy-start | bytes 772
  48.6 6.9 %collective-permute-start.1 = (f32[128,256]{1,0:T(8,128)S(1)}, f32[128,256]{1,0:T(8,128)S(1)}, u32[]{:S(2)}, u32[]{:S(2)}) collective-permute-start(f32[128,256]{1,0:T(8,128)S(1)} %shard_map.58.one_ref), channel_id=1, source_target_pairs={{0,2},{1,3},{2,0},{3,1},{4,6},{5,7},{6,4},{7,5},{8,10},{9,11},{10,... | collective-permute-start | bytes 393224 | tf_op jit(solution)/shard_map/ppermute | solution.py:295
  56.6 3.8 %collective-permute-start.3 = (f32[4,128,256]{2,1,0:T(8,128)S(1)}, f32[4,128,256]{2,1,0:T(8,128)S(1)}, u32[]{:S(2)}, u32[]{:S(2)}) collective-permute-start(f32[4,128,256]{2,1,0:T(8,128)S(1)} %get-tuple-element.26), channel_id=1, source_target_pairs={{0,1},{1,0},{2,3},{3,2},{4,5},{5,4},{6,7},{7,6},{8,9},{9,8},{10,11... | collective-permute-start | bytes 1572872 | tf_op jit(solution)/shard_map/ppermute | solution.py:295
  60.5 14.8 %collective-permute-start.5 = (f32[128,256]{1,0:T(8,128)S(1)}, f32[128,256]{1,0:T(8,128)S(1)}, u32[]{:S(2)}, u32[]{:S(2)}) collective-permute-start(f32[128,256]{1,0:T(8,128)S(1)} %get-tuple-element.30), channel_id=1, source_target_pairs={{0,4},{1,5},{2,6},{3,7},{4,0},{5,1},{6,2},{7,3},{8,12},{9,13},{10,... | collective-permute-start | bytes 393224 | tf_op jit(solution)/shard_map/ppermute | solution.py:295
  64.8 16.6 %collective-permute-start.4 = (f32[128,256]{1,0:T(8,128)S(1)}, f32[128,256]{1,0:T(8,128)S(1)}, u32[]{:S(2)}, u32[]{:S(2)}) collective-permute-start(f32[128,256]{1,0:T(8,128)S(1)} %get-tuple-element.28), channel_id=1, source_target_pairs={{0,4},{1,5},{2,6},{3,7},{4,0},{5,1},{6,2},{7,3},{8,12},{9,13},{10,... | collective-permute-start | bytes 393224 | tf_op jit(solution)/shard_map/ppermute | solution.py:295
  75.3 16.7 %collective-permute-start.6 = (f32[128,256]{1,0:T(8,128)S(1)}, f32[128,256]{1,0:T(8,128)S(1)}, u32[]{:S(2)}, u32[]{:S(2)}) collective-permute-start(f32[128,256]{1,0:T(8,128)S(1)} %shard_map.61), channel_id=1, source_target_pairs={{0,8},{1,9},{2,10},{3,11},{4,12},{5,13},{6,14},{7,15},{8,0},{9,1},... | collective-permute-start | bytes 393224 | tf_op jit(solution)/shard_map/ppermute | solution.py:295

commit v4 on v3

--- a/solution.py
+++ b/solution.py
@@ -223,13 +223,15 @@
             mate_ref[k, at, :] = total[(2 * k + 1) * cm:(2 * k + 2) * cm, :]
 
 
-def join_kernel(mine_ref, mate_ref, *outs):
-    for k, out in enumerate(outs):
-        out[...] = mine_ref[k] + mate_ref[k]
-
-
-def far_kernel(far_ref, got_ref, out_ref):
-    out_ref[...] = far_ref[...] + got_ref[...]
+def join_kernel(mine_ref, mate_ref, own_ref, far_ref, near_ref):
+    own_ref[...] = mine_ref[0] + mate_ref[0]
+    far_ref[...] = mine_ref[2] + mate_ref[2]
+    near_ref[0] = mine_ref[3] + mate_ref[3]
+    near_ref[1] = mine_ref[1] + mate_ref[1]
+
+
+def far_kernel(far_ref, near_ref, out_ref):
+    out_ref[...] = far_ref[...] + near_ref[0]
 
 
 def spread_kernel(oi, own_ref, near_ref, far_ref, occ_ref, vir_ref, out_ref):
@@ -240,7 +242,7 @@
     occ = occ_ref[...].astype(F32)
     irr_j = to_column(occ).astype(I32)
     sym_ab = pair_lanes(vcol, v * width, nvir, width)
-    total = (own_ref[...] + near_ref[...] + far_ref[...]).T
+    total = (own_ref[...] + near_ref[1] + far_ref[...]).T
     split = pieces(total, 3)
     n = total.shape[1]
     lane = iota((1, width * nvir), 1)
@@ -337,11 +339,12 @@
         2 * 10**9,
         interpret,
     )
-    sums = call(join_kernel, [one] * far, [mine, swap(mate, 1)], 10**6, interpret)
-    (far,) = call(far_kernel, [one], [sums[2], swap(sums[3], 4)], 10**6, interpret)
-    far, near = swap(far, 8), swap(sums[1], 4)
+    sums, far, near = call(join_kernel, [one, one, array(2, oi * cm, nocc)], [mine, swap(mate, 1)], 10**6, interpret)
+    near = swap(near, 4)
+    (far,) = call(far_kernel, [one], [far, near], 10**6, interpret)
+    far = swap(far, 8)
     (out,) = call(
-        functools.partial(spread_kernel, oi), [array(*amplitudes.shape)], [sums[0], near, far, occ, vir], 10**9, interpret
+        functools.partial(spread_kernel, oi), [array(*amplitudes.shape)], [sums, near, far, occ, vir], 10**9, interpret
     )
     return out
 

time: 94.1 us -> 98.5 us (1.047)
  the two profiles are of different devices: /device:TPU:8 before, /device:TPU:1 now
where the time goes in v4:
time: 98.5 us; the launch traced here: 98.2 us
  starting transfers between devices  51.2 us (52%)
  waiting for transfers between devices  34.6 us (35%)
  Pallas kernels  12.3 us (12%)
    ppermute x5, waiting for transfers between devices, swap(): return lax.ppermute(x, 'vir', [(i, i ^ k) for i in range(nvirdev)])  28.5 us
    ppermute x5, starting transfers between devices, swap(): return lax.ppermute(x, 'vir', [(i, i ^ k) for i in range(nvirdev)])  21.6 us
    ppermute x1, starting transfers between devices, body(): lax.ppermute(hop, 'occ', [(i, (i + devices // 2) % devices) for i in rang...  19.9 us
    pallas_call x8, Pallas kernels, call(): pl.pallas_call(kernel, out_shape=outs, in_specs=[spec(space)] * len(ins),...  12.3 us
    all_to_all x1, starting transfers between devices, body(): lax.all_to_all(send.reshape(devices // 2, 2 * oi, oi * cm), 'occ', 0, 0,...  9.67 us
    all_to_all x1, waiting for transfers between devices, body(): lax.all_to_all(send.reshape(devices // 2, 2 * oi, oi * cm), 'occ', 0, 0,...  6.07 us
  transfers between devices with their start and end apart: 7, of which 5 were waited for; matrix products, arithmetic and copies ran while one was open for 0% of the time, Pallas kernels for 6%

profile of v4, /device:TPU:1, one launch (start us, length us, event | category | flops | bytes accessed | tf_op | source)
XLA Modules:
  0.0 98.2 jit_solution(7762182241512703764)
XLA Ops:
  0.0 2.4 %shard_map.55 = (f32[256,128]{1,0:T(8,128)S(1)}, f32[128,128]{1,0:T(8,128)S(1)}, f32[128,128]{1,0:T(8,128)S(1)}) custom-call(f32[1024,256]{1,0:T(8,128)} %amp_hbm.1, s32[1,256]{1,0:T(1,128)} %bitcast.5, s32[1,64]{1,0:T(1,128)} %bitcast.8, s32[1,2]{1,0:T(1,128)} %tile_hbm.1), custom_call_target="tpu_custom_call" | custom-call | flops 1000000000 | bytes 1312008 | tf_op jit(solution)/shard_map/pallas_call | solution.py:266
  2.5 0.0 copy-start
  2.5 19.9 %collective-permute-start = (f32[128,128]{1,0:T(8,128)S(1)}, f32[128,128]{1,0:T(8,128)S(1)}, u32[]{:S(2)}, u32[]{:S(2)}) collective-permute-start(f32[128,128]{1,0:T(8,128)S(1)} %get-tuple-element.21), channel_id=1, source_target_pairs={{0,512},{16,528},{32,544},{48,560},{64,576},{80,592},{96,608},{112... | collective-permute-start | bytes 196616 | tf_op jit(solution)/shard_map/ppermute | solution.py:311
  22.4 6.1 %shard_map.56 = (f32[256,256]{1,0:T(8,128)S(1)}, f32[256,256]{1,0:T(8,128)S(1)}) custom-call(f32[256,4096]{1,0:T(8,128)} %int_hbm.1, s32[1,64]{1,0:T(1,128)} %bitcast.9), custom_call_target="tpu_custom_call" | custom-call | flops 4000000000 | bytes 4718848 | tf_op jit(solution)/shard_map/pallas_call | solution.py:266
  28.5 0.0 collective-permute-done.hop_ref
  28.5 0.7 shard_map.57
  29.2 9.7 %all-to-all-start = ((f32[32,8,128]{2,1,0:T(8,128)}), f32[32,8,128]{2,1,0:T(8,128)S(1)}, u32[]{:S(2)}, u32[]{:S(2)}) async-start(f32[32,8,128]{2,1,0:T(8,128)} %bitcast.2), calls=%async_computation | async-start | bytes 262144 | tf_op jit(solution)/shard_map/all_to_all | solution.py:327
  38.9 3.1 %collective-permute-start.2 = (f32[256,256]{1,0:T(8,128)S(1)}, f32[256,256]{1,0:T(8,128)S(1)}, u32[]{:S(2)}, u32[]{:S(2)}) collective-permute-start(f32[256,256]{1,0:T(8,128)S(1)} %get-tuple-element.23), channel_id=1, source_target_pairs={{0,2},{1,3},{2,0},{3,1},{4,6},{5,7},{6,4},{7,5},{8,10},{9,11},{10,... | collective-permute-start | bytes 786440 | tf_op jit(solution)/shard_map/ppermute | solution.py:297
  42.0 6.1 %all-to-all-done = f32[32,8,128]{2,1,0:T(8,128)S(1)} async-done(((f32[32,8,128]{2,1,0:T(8,128)}), f32[32,8,128]{2,1,0:T(8,128)S(1)}, u32[]{:S(2)}, u32[]{:S(2)}) %all-to-all-start) | async-done | bytes 131104 | tf_op jit(solution)/shard_map/all_to_all | solution.py:327
  48.1 0.1 shard_map.58.one_ref
  48.2 0.0 copy-start.1
  48.2 3.1 %collective-permute-start.1 = (f32[128,256]{1,0:T(8,128)S(1)}, f32[128,256]{1,0:T(8,128)S(1)}, u32[]{:S(2)}, u32[]{:S(2)}) collective-permute-start(f32[128,256]{1,0:T(8,128)S(1)} %shard_map.58.one_ref), channel_id=1, source_target_pairs={{0,2},{1,3},{2,0},{3,1},{4,6},{5,7},{6,4},{7,5},{8,10},{9,11},{10,... | collective-permute-start | bytes 393224 | tf_op jit(solution)/shard_map/ppermute | solution.py:297
  51.3 0.0 collective-permute-done.2.got_ref
  51.3 2.6 %collective-permute-done.1.two_ref = f32[128,256]{1,0:T(8,128)S(1)} collective-permute-done((f32[128,256]{1,0:T(8,128)S(1)}, f32[128,256]{1,0:T(8,128)S(1)}, u32[]{:S(2)}, u32[]{:S(2)}) %collective-permute-start.1) | collective-permute-done | bytes 131104 | tf_op jit(solution)/shard_map/ppermute | solution.py:297
  53.9 0.0 copy-done
  53.9 1.1 %shard_map.59 = (f32[4,128,256]{2,1,0:T(8,128)S(1)}, f32[4,128,256]{2,1,0:T(8,128)S(1)}) custom-call(f32[128,256]{1,0:T(8,128)S(1)} %shard_map.58.one_ref, f32[128,256]{1,0:T(8,128)S(1)} %collective-permute-done.1.two_ref, f32[256,256]{1,0:T(8,128)S(1)} %get-tuple-element.22.keep_ref, f32[256,256]{1,0:T(8,128)S(1)} %collective-permute-done.2.got_ref, ...), custom_call_target="tpu_custom_call" | custom-call | flops 2000000000 | bytes 1836032 | tf_op jit(solution)/shard_map/pallas_call | solution.py:266
  55.0 5.4 %collective-permute-start.3 = (f32[4,128,256]{2,1,0:T(8,128)S(1)}, f32[4,128,256]{2,1,0:T(8,128)S(1)}, u32[]{:S(2)}, u32[]{:S(2)}) collective-permute-start(f32[4,128,256]{2,1,0:T(8,128)S(1)} %get-tuple-element.25), channel_id=1, source_target_pairs={{0,1},{1,0},{2,3},{3,2},{4,5},{5,4},{6,7},{7,6},{8,9},{9,8},{10,11... | collective-permute-start | bytes 1572872 | tf_op jit(solution)/shard_map/ppermute | solution.py:297
  60.5 1.5 %collective-permute-done.3.mate_ref = f32[4,128,256]{2,1,0:T(8,128)S(1)} collective-permute-done((f32[4,128,256]{2,1,0:T(8,128)S(1)}, f32[4,128,256]{2,1,0:T(8,128)S(1)}, u32[]{:S(2)}, u32[]{:S(2)}) %collective-permute-start.3) | collective-permute-done | bytes 524320 | tf_op jit(solution)/shard_map/ppermute | solution.py:297
  62.0 0.1 shard_map.60
  62.0 4.0 %collective-permute-start.4 = (f32[2,128,256]{2,1,0:T(8,128)S(1)}, f32[2,128,256]{2,1,0:T(8,128)S(1)}, u32[]{:S(2)}, u32[]{:S(2)}) collective-permute-start(f32[2,128,256]{2,1,0:T(8,128)S(1)} %get-tuple-element.27), channel_id=1, source_target_pairs={{0,4},{1,5},{2,6},{3,7},{4,0},{5,1},{6,2},{7,3},{8,12},{9,13},{10,... | collective-permute-start | bytes 786440 | tf_op jit(solution)/shard_map/ppermute | solution.py:297
  66.0 11.9 %collective-permute-done.4.near_ref = f32[2,128,256]{2,1,0:T(8,128)S(1)} collective-permute-done((f32[2,128,256]{2,1,0:T(8,128)S(1)}, f32[2,128,256]{2,1,0:T(8,128)S(1)}, u32[]{:S(2)}, u32[]{:S(2)}) %collective-permute-start.4) | collective-permute-done | bytes 262176 | tf_op jit(solution)/shard_map/ppermute | solution.py:297
  78.0 6.0 %collective-permute-start.5 = (f32[128,256]{1,0:T(8,128)S(1)}, f32[128,256]{1,0:T(8,128)S(1)}, u32[]{:S(2)}, u32[]{:S(2)}) collective-permute-start(f32[128,256]{1,0:T(8,128)S(1)} %shard_map.61), channel_id=1, source_target_pairs={{0,8},{1,9},{2,10},{3,11},{4,12},{5,13},{6,14},{7,15},{8,0},{9,1},... | collective-permute-start | bytes 393224 | tf_op jit(solution)/shard_map/ppermute | solution.py:297
  84.0 12.5 %collective-permute-done.5.far_ref = f32[128,256]{1,0:T(8,128)S(1)} collective-permute-done((f32[128,256]{1,0:T(8,128)S(1)}, f32[128,256]{1,0:T(8,128)S(1)}, u32[]{:S(2)}, u32[]{:S(2)}) %collective-permute-start.5) | collective-permute-done | bytes 131104 | tf_op jit(solution)/shard_map/ppermute | solution.py:297
  96.5 0.0 copy-done.1
  96.5 1.7 %shard_map.62 = f32[1024,256]{1,0:T(8,128)} custom-call(f32[128,256]{1,0:T(8,128)S(1)} %get-tuple-element.26.own_ref, f32[2,128,256]{2,1,0:T(8,128)S(1)} %collective-permute-done.4.near_ref, f32[128,256]{1,0:T(8,128)S(1)} %collective-permute-done.5.far_ref, s32[1,256]{1,0:T(1,128)S(1)} %bitcast.7, s32[1,64]{1,0:T(1,128)S(1)} %bitcast.10), custom_call_target="tpu_custom_call" | custom-call | flops 1000000000 | bytes 1574144 | tf_op jit(solution)/shard_map/pallas_call | solution.py:266
  (1 shorter events, 0.0 us)
Async XLA Ops:
  2.5 51.5 %copy-start = (s32[256]{0:T(256)S(1)}, s32[256]{0:T(256)}, u32[]{:S(2)}) copy-start(s32[256]{0:T(256)} %param.7) | copy-start | bytes 3076
  2.5 26.0 %collective-permute-start = (f32[128,128]{1,0:T(8,128)S(1)}, f32[128,128]{1,0:T(8,128)S(1)}, u32[]{:S(2)}, u32[]{:S(2)}) collective-permute-start(f32[128,128]{1,0:T(8,128)S(1)} %get-tuple-element.21), channel_id=1, source_target_pairs={{0,512},{16,528},{32,544},{48,560},{64,576},{80,592},{96,608},{112... | collective-permute-start | bytes 196616 | tf_op jit(solution)/shard_map/ppermute | solution.py:311
  29.2 18.9 %all-to-all-start = ((f32[32,8,128]{2,1,0:T(8,128)}), f32[32,8,128]{2,1,0:T(8,128)S(1)}, u32[]{:S(2)}, u32[]{:S(2)}) async-start(f32[32,8,128]{2,1,0:T(8,128)} %bitcast.2), calls=%async_computation | async-start | bytes 262144 | tf_op jit(solution)/shard_map/all_to_all | solution.py:327
  38.9 12.4 %collective-permute-start.2 = (f32[256,256]{1,0:T(8,128)S(1)}, f32[256,256]{1,0:T(8,128)S(1)}, u32[]{:S(2)}, u32[]{:S(2)}) collective-permute-start(f32[256,256]{1,0:T(8,128)S(1)} %get-tuple-element.23), channel_id=1, source_target_pairs={{0,2},{1,3},{2,0},{3,1},{4,6},{5,7},{6,4},{7,5},{8,10},{9,11},{10,... | collective-permute-start | bytes 786440 | tf_op jit(solution)/shard_map/ppermute | solution.py:297
  48.2 48.3 %copy-start.1 = (s32[64]{0:T(128)S(1)}, s32[64]{0:T(128)}, u32[]{:S(2)}) copy-start(s32[64]{0:T(128)} %param.8) | copy-start | bytes 772
  48.2 5.7 %collective-permute-start.1 = (f32[128,256]{1,0:T(8,128)S(1)}, f32[128,256]{1,0:T(8,128)S(1)}, u32[]{:S(2)}, u32[]{:S(2)}) collective-permute-start(f32[128,256]{1,0:T(8,128)S(1)} %shard_map.58.one_ref), channel_id=1, source_target_pairs={{0,2},{1,3},{2,0},{3,1},{4,6},{5,7},{6,4},{7,5},{8,10},{9,11},{10,... | collective-permute-start | bytes 393224 | tf_op jit(solution)/shard_map/ppermute | solution.py:297
  55.0 6.9 %collective-permute-start.3 = (f32[4,128,256]{2,1,0:T(8,128)S(1)}, f32[4,128,256]{2,1,0:T(8,128)S(1)}, u32[]{:S(2)}, u32[]{:S(2)}) collective-permute-start(f32[4,128,256]{2,1,0:T(8,128)S(1)} %get-tuple-element.25), channel_id=1, source_target_pairs={{0,1},{1,0},{2,3},{3,2},{4,5},{5,4},{6,7},{7,6},{8,9},{9,8},{10,11... | collective-permute-start | bytes 1572872 | tf_op jit(solution)/shard_map/ppermute | solution.py:297
  62.0 15.9 %collective-permute-start.4 = (f32[2,128,256]{2,1,0:T(8,128)S(1)}, f32[2,128,256]{2,1,0:T(8,128)S(1)}, u32[]{:S(2)}, u32[]{:S(2)}) collective-permute-start(f32[2,128,256]{2,1,0:T(8,128)S(1)} %get-tuple-element.27), channel_id=1, source_target_pairs={{0,4},{1,5},{2,6},{3,7},{4,0},{5,1},{6,2},{7,3},{8,12},{9,13},{10,... | collective-permute-start | bytes 786440 | tf_op jit(solution)/shard_map/ppermute | solution.py:297
  78.0 18.5 %collective-permute-start.5 = (f32[128,256]{1,0:T(8,128)S(1)}, f32[128,256]{1,0:T(8,128)S(1)}, u32[]{:S(2)}, u32[]{:S(2)}) collective-permute-start(f32[128,256]{1,0:T(8,128)S(1)} %shard_map.61), channel_id=1, source_target_pairs={{0,8},{1,9},{2,10},{3,11},{4,12},{5,13},{6,14},{7,15},{8,0},{9,1},... | collective-permute-start | bytes 393224 | tf_op jit(solution)/shard_map/ppermute | solution.py:297

commit v5 on v3

--- a/solution.py
+++ b/solution.py
@@ -197,16 +197,17 @@
     out_ref[...] = diff_ref[...].T
 
 
-def ladder_kernel(oi, one_ref, two_ref, keep_ref, got_ref, occ_ref, mine_ref, mate_ref):
+def ladder_kernel(oi, part, one_ref, two_ref, keep_ref, got_ref, occ_ref, *refs):
+    mine_ref, mate_ref = refs[-2:]
     nocc = occ_ref.shape[1]
     o = lax.axis_index("occ")
     occ = occ_ref[...].astype(F32)
     cm = one_ref.shape[0] // oi
+    n = keep_ref.shape[0] // 2
     stacked = []
     for ref in (keep_ref, got_ref):
-        high, low = pieces(ref[...], 2)
+        high, low = pieces(ref[part * n:(part + 1) * n, :], 2)
         stacked.append((jnp.concatenate([high, low], axis=0), high))
-    n = keep_ref.shape[0]
     for ii in range(oi):
         irr_i = pick_rows(occ, jnp.full((1, 1), o * oi + ii, I32)).astype(I32)
         sym = jnp.bitwise_xor(occ_ref[...], irr_i)
@@ -329,19 +330,16 @@
     one = array(oi * cm, nocc)
     scratch = [pltpu.VMEM((nocc, oi * cm), F32)]
     (anti,) = call(functools.partial(antisym_kernel, oi), [one], [own, got], 10**6, interpret, scratch=scratch)
-    far = nvirdev // 4
-    mine, mate = call(
-        functools.partial(ladder_kernel, oi),
-        [array(far, oi * cm, nocc)] * 2,
-        [anti, swap(anti, 2), keep, given, occ],
-        2 * 10**9,
-        interpret,
-    )
-    sums = call(join_kernel, [one] * far, [mine, swap(mate, 1)], 10**6, interpret)
-    (far,) = call(far_kernel, [one], [sums[2], swap(sums[3], 4)], 10**6, interpret)
-    far, near = swap(far, 8), swap(sums[1], 4)
+    pair = [anti, swap(anti, 2), keep, given, occ]
+    two = [array(2, oi * cm, nocc)] * 2
+    mine, mate = call(functools.partial(ladder_kernel, oi, 1), two, pair, 10**9, interpret)
+    far, farther = call(join_kernel, [one] * 2, [mine, swap(mate, 1)], 10**6, interpret)
+    mine, mate = call(functools.partial(ladder_kernel, oi, 0), two, [*pair, far], 10**9, interpret)
+    total, near = call(join_kernel, [one] * 2, [mine, swap(mate, 1)], 10**6, interpret)
+    (far,) = call(far_kernel, [one], [far, swap(farther, 4)], 10**6, interpret)
+    far, near = swap(far, 8), swap(near, 4)
     (out,) = call(
-        functools.partial(spread_kernel, oi), [array(*amplitudes.shape)], [sums[0], near, far, occ, vir], 10**9, interpret
+        functools.partial(spread_kernel, oi), [array(*amplitudes.shape)], [total, near, far, occ, vir], 10**9, interpret
     )
     return out
 

time: 94.1 us -> 98.2 us (1.044)
  the two profiles are of different devices: /device:TPU:8 before, /device:TPU:1 now
where the time goes in v5:
time: 98.2 us; the launch traced here: 97.8 us
  starting transfers between devices  55.4 us (56%)
  waiting for transfers between devices  29.6 us (30%)
  Pallas kernels  12.6 us (13%)
    ppermute x7, starting transfers between devices, swap(): return lax.ppermute(x, 'vir', [(i, i ^ k) for i in range(nvirdev)])  25.8 us
    ppermute x7, waiting for transfers between devices, swap(): return lax.ppermute(x, 'vir', [(i, i ^ k) for i in range(nvirdev)])  23.5 us
    ppermute x1, starting transfers between devices, body(): lax.ppermute(hop, 'occ', [(i, (i + devices // 2) % devices) for i in rang...  19.9 us
    pallas_call x10, Pallas kernels, call(): pl.pallas_call(kernel, out_shape=outs, in_specs=[spec(space)] * len(ins),...  12.6 us
    all_to_all x1, starting transfers between devices, body(): lax.all_to_all(send.reshape(devices // 2, 2 * oi, oi * cm), 'occ', 0, 0,...  9.67 us
    all_to_all x1, waiting for transfers between devices, body(): lax.all_to_all(send.reshape(devices // 2, 2 * oi, oi * cm), 'occ', 0, 0,...  6.07 us
  transfers between devices with their start and end apart: 9, of which 6 were waited for; matrix products, arithmetic and copies ran while one was open for 0% of the time, Pallas kernels for 6%

profile of v5, /device:TPU:1, one launch (start us, length us, event | category | flops | bytes accessed | tf_op | source)
XLA Modules:
  0.0 97.8 jit_solution(16509417013005283512)
XLA Ops:
  0.0 2.4 %shard_map.55 = (f32[256,128]{1,0:T(8,128)S(1)}, f32[128,128]{1,0:T(8,128)S(1)}, f32[128,128]{1,0:T(8,128)S(1)}) custom-call(f32[1024,256]{1,0:T(8,128)} %amp_hbm.1, s32[1,256]{1,0:T(1,128)} %bitcast.5, s32[1,64]{1,0:T(1,128)} %bitcast.9, s32[1,2]{1,0:T(1,128)} %tile_hbm.1), custom_call_target="tpu_custom_call" | custom-call | flops 1000000000 | bytes 1312008 | tf_op jit(solution)/shard_map/pallas_call | solution.py:265
  2.5 0.0 copy-start
  2.5 19.9 %collective-permute-start = (f32[128,128]{1,0:T(8,128)S(1)}, f32[128,128]{1,0:T(8,128)S(1)}, u32[]{:S(2)}, u32[]{:S(2)}) collective-permute-start(f32[128,128]{1,0:T(8,128)S(1)} %get-tuple-element.24), channel_id=1, source_target_pairs={{0,512},{16,528},{32,544},{48,560},{64,576},{80,592},{96,608},{112... | collective-permute-start | bytes 196616 | tf_op jit(solution)/shard_map/ppermute | solution.py:310
  22.4 6.1 %shard_map.56 = (f32[256,256]{1,0:T(8,128)S(1)}, f32[256,256]{1,0:T(8,128)S(1)}) custom-call(f32[256,4096]{1,0:T(8,128)} %int_hbm.1, s32[1,64]{1,0:T(1,128)} %bitcast.10), custom_call_target="tpu_custom_call" | custom-call | flops 4000000000 | bytes 4718848 | tf_op jit(solution)/shard_map/pallas_call | solution.py:265
  28.5 0.0 collective-permute-done.hop_ref
  28.5 0.7 shard_map.57
  29.2 9.7 %all-to-all-start = ((f32[32,8,128]{2,1,0:T(8,128)}), f32[32,8,128]{2,1,0:T(8,128)S(1)}, u32[]{:S(2)}, u32[]{:S(2)}) async-start(f32[32,8,128]{2,1,0:T(8,128)} %bitcast.2), calls=%async_computation | async-start | bytes 262144 | tf_op jit(solution)/shard_map/all_to_all | solution.py:326
  38.9 3.1 %collective-permute-start.2 = (f32[256,256]{1,0:T(8,128)S(1)}, f32[256,256]{1,0:T(8,128)S(1)}, u32[]{:S(2)}, u32[]{:S(2)}) collective-permute-start(f32[256,256]{1,0:T(8,128)S(1)} %get-tuple-element.26), channel_id=1, source_target_pairs={{0,2},{1,3},{2,0},{3,1},{4,6},{5,7},{6,4},{7,5},{8,10},{9,11},{10,... | collective-permute-start | bytes 786440 | tf_op jit(solution)/shard_map/ppermute | solution.py:296
  42.0 6.1 %all-to-all-done = f32[32,8,128]{2,1,0:T(8,128)S(1)} async-done(((f32[32,8,128]{2,1,0:T(8,128)}), f32[32,8,128]{2,1,0:T(8,128)S(1)}, u32[]{:S(2)}, u32[]{:S(2)}) %all-to-all-start) | async-done | bytes 131104 | tf_op jit(solution)/shard_map/all_to_all | solution.py:326
  48.1 0.1 shard_map.58.one_ref
  48.2 0.0 copy-start.1
  48.2 3.1 %collective-permute-start.1 = (f32[128,256]{1,0:T(8,128)S(1)}, f32[128,256]{1,0:T(8,128)S(1)}, u32[]{:S(2)}, u32[]{:S(2)}) collective-permute-start(f32[128,256]{1,0:T(8,128)S(1)} %shard_map.58.one_ref), channel_id=1, source_target_pairs={{0,2},{1,3},{2,0},{3,1},{4,6},{5,7},{6,4},{7,5},{8,10},{9,11},{10,... | collective-permute-start | bytes 393224 | tf_op jit(solution)/shard_map/ppermute | solution.py:296
  51.3 0.0 collective-permute-done.2.got_ref
  51.3 2.6 %collective-permute-done.1.two_ref = f32[128,256]{1,0:T(8,128)S(1)} collective-permute-done((f32[128,256]{1,0:T(8,128)S(1)}, f32[128,256]{1,0:T(8,128)S(1)}, u32[]{:S(2)}, u32[]{:S(2)}) %collective-permute-start.1) | collective-permute-done | bytes 131104 | tf_op jit(solution)/shard_map/ppermute | solution.py:296
  53.9 0.0 copy-done
  53.9 0.7 shard_map.59
  54.7 5.4 %collective-permute-start.3 = (f32[2,128,256]{2,1,0:T(8,128)S(1)}, f32[2,128,256]{2,1,0:T(8,128)S(1)}, u32[]{:S(2)}, u32[]{:S(2)}) collective-permute-start(f32[2,128,256]{2,1,0:T(8,128)S(1)} %get-tuple-element.28), channel_id=1, source_target_pairs={{0,1},{1,0},{2,3},{3,2},{4,5},{5,4},{6,7},{7,6},{8,9},{9,8},{10,11... | collective-permute-start | bytes 786440 | tf_op jit(solution)/shard_map/ppermute | solution.py:296
  60.1 1.1 %collective-permute-done.3.mate_ref = f32[2,128,256]{2,1,0:T(8,128)S(1)} collective-permute-done((f32[2,128,256]{2,1,0:T(8,128)S(1)}, f32[2,128,256]{2,1,0:T(8,128)S(1)}, u32[]{:S(2)}, u32[]{:S(2)}) %collective-permute-start.3) | collective-permute-done | bytes 262176 | tf_op jit(solution)/shard_map/ppermute | solution.py:296
  61.3 0.8 shard_map.61
  62.0 2.3 %collective-permute-start.4 = (f32[2,128,256]{2,1,0:T(8,128)S(1)}, f32[2,128,256]{2,1,0:T(8,128)S(1)}, u32[]{:S(2)}, u32[]{:S(2)}) collective-permute-start(f32[2,128,256]{2,1,0:T(8,128)S(1)} %get-tuple-element.31), channel_id=1, source_target_pairs={{0,1},{1,0},{2,3},{3,2},{4,5},{5,4},{6,7},{7,6},{8,9},{9,8},{10,11... | collective-permute-start | bytes 786440 | tf_op jit(solution)/shard_map/ppermute | solution.py:296
  64.3 4.0 %collective-permute-start.6 = (f32[128,256]{1,0:T(8,128)S(1)}, f32[128,256]{1,0:T(8,128)S(1)}, u32[]{:S(2)}, u32[]{:S(2)}) collective-permute-start(f32[128,256]{1,0:T(8,128)S(1)} %get-tuple-element.34), channel_id=1, source_target_pairs={{0,4},{1,5},{2,6},{3,7},{4,0},{5,1},{6,2},{7,3},{8,12},{9,13},{10,... | collective-permute-start | bytes 393224 | tf_op jit(solution)/shard_map/ppermute | solution.py:296
  68.3 6.5 %collective-permute-done.6.got_ref = f32[128,256]{1,0:T(8,128)S(1)} collective-permute-done((f32[128,256]{1,0:T(8,128)S(1)}, f32[128,256]{1,0:T(8,128)S(1)}, u32[]{:S(2)}, u32[]{:S(2)}) %collective-permute-start.6) | collective-permute-done | bytes 131104 | tf_op jit(solution)/shard_map/ppermute | solution.py:296
  74.9 6.0 %collective-permute-start.7 = (f32[128,256]{1,0:T(8,128)S(1)}, f32[128,256]{1,0:T(8,128)S(1)}, u32[]{:S(2)}, u32[]{:S(2)}) collective-permute-start(f32[128,256]{1,0:T(8,128)S(1)} %shard_map.63), channel_id=1, source_target_pairs={{0,8},{1,9},{2,10},{3,11},{4,12},{5,13},{6,14},{7,15},{8,0},{9,1},... | collective-permute-start | bytes 393224 | tf_op jit(solution)/shard_map/ppermute | solution.py:296
  80.8 0.0 collective-permute-done.4.mate_ref
  80.9 1.9 %collective-permute-start.5 = (f32[128,256]{1,0:T(8,128)S(1)}, f32[128,256]{1,0:T(8,128)S(1)}, u32[]{:S(2)}, u32[]{:S(2)}) collective-permute-start(f32[128,256]{1,0:T(8,128)S(1)} %get-tuple-element.33), channel_id=1, source_target_pairs={{0,4},{1,5},{2,6},{3,7},{4,0},{5,1},{6,2},{7,3},{8,12},{9,13},{10,... | collective-permute-start | bytes 393224 | tf_op jit(solution)/shard_map/ppermute | solution.py:296
  82.8 10.8 %collective-permute-done.7.far_ref = f32[128,256]{1,0:T(8,128)S(1)} collective-permute-done((f32[128,256]{1,0:T(8,128)S(1)}, f32[128,256]{1,0:T(8,128)S(1)}, u32[]{:S(2)}, u32[]{:S(2)}) %collective-permute-start.7) | collective-permute-done | bytes 131104 | tf_op jit(solution)/shard_map/ppermute | solution.py:296
  93.6 2.4 %collective-permute-done.5.near_ref = f32[128,256]{1,0:T(8,128)S(1)} collective-permute-done((f32[128,256]{1,0:T(8,128)S(1)}, f32[128,256]{1,0:T(8,128)S(1)}, u32[]{:S(2)}, u32[]{:S(2)}) %collective-permute-start.5) | collective-permute-done | bytes 131104 | tf_op jit(solution)/shard_map/ppermute | solution.py:296
  96.0 0.0 copy-done.1
  96.1 1.7 %shard_map.64 = f32[1024,256]{1,0:T(8,128)} custom-call(f32[128,256]{1,0:T(8,128)S(1)} %get-tuple-element.32.own_ref, f32[128,256]{1,0:T(8,128)S(1)} %collective-permute-done.5.near_ref, f32[128,256]{1,0:T(8,128)S(1)} %collective-permute-done.7.far_ref, s32[1,256]{1,0:T(1,128)S(1)} %bitcast.8, s32[1,64]{1,0:T(1,128)S(1)} %bitcast.11), custom_call_target="tpu_custom_call" | custom-call | flops 1000000000 | bytes 1443072 | tf_op jit(solution)/shard_map/pallas_call | solution.py:265
  (3 shorter events, 0.1 us)
Async XLA Ops:
  2.5 51.5 %copy-start = (s32[256]{0:T(256)S(1)}, s32[256]{0:T(256)}, u32[]{:S(2)}) copy-start(s32[256]{0:T(256)} %param.7) | copy-start | bytes 3076
  2.5 26.0 %collective-permute-start = (f32[128,128]{1,0:T(8,128)S(1)}, f32[128,128]{1,0:T(8,128)S(1)}, u32[]{:S(2)}, u32[]{:S(2)}) collective-permute-start(f32[128,128]{1,0:T(8,128)S(1)} %get-tuple-element.24), channel_id=1, source_target_pairs={{0,512},{16,528},{32,544},{48,560},{64,576},{80,592},{96,608},{112... | collective-permute-start | bytes 196616 | tf_op jit(solution)/shard_map/ppermute | solution.py:310
  29.2 18.9 %all-to-all-start = ((f32[32,8,128]{2,1,0:T(8,128)}), f32[32,8,128]{2,1,0:T(8,128)S(1)}, u32[]{:S(2)}, u32[]{:S(2)}) async-start(f32[32,8,128]{2,1,0:T(8,128)} %bitcast.2), calls=%async_computation | async-start | bytes 262144 | tf_op jit(solution)/shard_map/all_to_all | solution.py:326
  38.9 12.4 %collective-permute-start.2 = (f32[256,256]{1,0:T(8,128)S(1)}, f32[256,256]{1,0:T(8,128)S(1)}, u32[]{:S(2)}, u32[]{:S(2)}) collective-permute-start(f32[256,256]{1,0:T(8,128)S(1)} %get-tuple-element.26), channel_id=1, source_target_pairs={{0,2},{1,3},{2,0},{3,1},{4,6},{5,7},{6,4},{7,5},{8,10},{9,11},{10,... | collective-permute-start | bytes 786440 | tf_op jit(solution)/shard_map/ppermute | solution.py:296
  48.2 47.9 %copy-start.1 = (s32[64]{0:T(128)S(1)}, s32[64]{0:T(128)}, u32[]{:S(2)}) copy-start(s32[64]{0:T(128)} %param.8) | copy-start | bytes 772
  48.2 5.7 %collective-permute-start.1 = (f32[128,256]{1,0:T(8,128)S(1)}, f32[128,256]{1,0:T(8,128)S(1)}, u32[]{:S(2)}, u32[]{:S(2)}) collective-permute-start(f32[128,256]{1,0:T(8,128)S(1)} %shard_map.58.one_ref), channel_id=1, source_target_pairs={{0,2},{1,3},{2,0},{3,1},{4,6},{5,7},{6,4},{7,5},{8,10},{9,11},{10,... | collective-permute-start | bytes 393224 | tf_op jit(solution)/shard_map/ppermute | solution.py:296
  54.7 6.6 %collective-permute-start.3 = (f32[2,128,256]{2,1,0:T(8,128)S(1)}, f32[2,128,256]{2,1,0:T(8,128)S(1)}, u32[]{:S(2)}, u32[]{:S(2)}) collective-permute-start(f32[2,128,256]{2,1,0:T(8,128)S(1)} %get-tuple-element.28), channel_id=1, source_target_pairs={{0,1},{1,0},{2,3},{3,2},{4,5},{5,4},{6,7},{7,6},{8,9},{9,8},{10,11... | collective-permute-start | bytes 786440 | tf_op jit(solution)/shard_map/ppermute | solution.py:296
  62.0 18.8 %collective-permute-start.4 = (f32[2,128,256]{2,1,0:T(8,128)S(1)}, f32[2,128,256]{2,1,0:T(8,128)S(1)}, u32[]{:S(2)}, u32[]{:S(2)}) collective-permute-start(f32[2,128,256]{2,1,0:T(8,128)S(1)} %get-tuple-element.31), channel_id=1, source_target_pairs={{0,1},{1,0},{2,3},{3,2},{4,5},{5,4},{6,7},{7,6},{8,9},{9,8},{10,11... | collective-permute-start | bytes 786440 | tf_op jit(solution)/shard_map/ppermute | solution.py:296
  64.3 10.6 %collective-permute-start.6 = (f32[128,256]{1,0:T(8,128)S(1)}, f32[128,256]{1,0:T(8,128)S(1)}, u32[]{:S(2)}, u32[]{:S(2)}) collective-permute-start(f32[128,256]{1,0:T(8,128)S(1)} %get-tuple-element.34), channel_id=1, source_target_pairs={{0,4},{1,5},{2,6},{3,7},{4,0},{5,1},{6,2},{7,3},{8,12},{9,13},{10,... | collective-permute-start | bytes 393224 | tf_op jit(solution)/shard_map/ppermute | solution.py:296
  74.9 18.7 %collective-permute-start.7 = (f32[128,256]{1,0:T(8,128)S(1)}, f32[128,256]{1,0:T(8,128)S(1)}, u32[]{:S(2)}, u32[]{:S(2)}) collective-permute-start(f32[128,256]{1,0:T(8,128)S(1)} %shard_map.63), channel_id=1, source_target_pairs={{0,8},{1,9},{2,10},{3,11},{4,12},{5,13},{6,14},{7,15},{8,0},{9,1},... | collective-permute-start | bytes 393224 | tf_op jit(solution)/shard_map/ppermute | solution.py:296
  80.9 15.2 %collective-permute-start.5 = (f32[128,256]{1,0:T(8,128)S(1)}, f32[128,256]{1,0:T(8,128)S(1)}, u32[]{:S(2)}, u32[]{:S(2)}) collective-permute-start(f32[128,256]{1,0:T(8,128)S(1)} %get-tuple-element.33), channel_id=1, source_target_pairs={{0,4},{1,5},{2,6},{3,7},{4,0},{5,1},{6,2},{7,3},{8,12},{9,13},{10,... | collective-permute-start | bytes 393224 | tf_op jit(solution)/shard_map/ppermute | solution.py:296

commit v6 on v3

--- a/solution.py
+++ b/solution.py
@@ -232,6 +232,11 @@
     out_ref[...] = far_ref[...] + got_ref[...]
 
 
+def near_kernel(near_ref, after_ref, out_ref):
+    del after_ref
+    out_ref[...] = near_ref[...]
+
+
 def spread_kernel(oi, own_ref, near_ref, far_ref, occ_ref, vir_ref, out_ref):
     nocc, nvir = occ_ref.shape[1], vir_ref.shape[1]
     width = out_ref.shape[1] // nvir
@@ -339,7 +344,8 @@
     )
     sums = call(join_kernel, [one] * far, [mine, swap(mate, 1)], 10**6, interpret)
     (far,) = call(far_kernel, [one], [sums[2], swap(sums[3], 4)], 10**6, interpret)
-    far, near = swap(far, 8), swap(sums[1], 4)
+    (near,) = call(near_kernel, [one], [sums[1], far], 10**10, interpret)
+    far, near = swap(far, 8), swap(near, 4)
     (out,) = call(
         functools.partial(spread_kernel, oi), [array(*amplitudes.shape)], [sums[0], near, far, occ, vir], 10**9, interpret
     )

time: 94.1 us -> 95 us (level)
  the two profiles are of different devices: /device:TPU:8 before, /device:TPU:65 now
where the time goes in v6:
time: 95 us; the launch traced here: 94.7 us
  starting transfers between devices  52.2 us (55%)
  waiting for transfers between devices  30 us (32%)
  Pallas kernels  12.3 us (13%)
    ppermute x6, starting transfers between devices, swap(): return lax.ppermute(x, 'vir', [(i, i ^ k) for i in range(nvirdev)])  24.3 us
    ppermute x6, waiting for transfers between devices, swap(): return lax.ppermute(x, 'vir', [(i, i ^ k) for i in range(nvirdev)])  23 us
    ppermute x1, starting transfers between devices, body(): lax.ppermute(hop, 'occ', [(i, (i + devices // 2) % devices) for i in rang...  18.2 us
    pallas_call x9, Pallas kernels, call(): pl.pallas_call(kernel, out_shape=outs, in_specs=[spec(space)] * len(ins),...  12.3 us
    all_to_all x1, starting transfers between devices, body(): lax.all_to_all(send.reshape(devices // 2, 2 * oi, oi * cm), 'occ', 0, 0,...  9.67 us
    all_to_all x1, waiting for transfers between devices, body(): lax.all_to_all(send.reshape(devices // 2, 2 * oi, oi * cm), 'occ', 0, 0,...  6.98 us
  transfers between devices with their start and end apart: 8, of which 5 were waited for; matrix products, arithmetic and copies ran while one was open for 0% of the time, Pallas kernels for 7%

profile of v6, /device:TPU:65, one launch (start us, length us, event | category | flops | bytes accessed | tf_op | source)
XLA Modules:
  0.0 94.7 jit_solution(15591895564458798607)
XLA Ops:
  0.0 2.4 %shard_map.55 = (f32[256,128]{1,0:T(8,128)S(1)}, f32[128,128]{1,0:T(8,128)S(1)}, f32[128,128]{1,0:T(8,128)S(1)}) custom-call(f32[1024,256]{1,0:T(8,128)} %amp_hbm.1, s32[1,256]{1,0:T(1,128)} %bitcast.5, s32[1,64]{1,0:T(1,128)} %bitcast.8, s32[1,2]{1,0:T(1,128)} %tile_hbm.1), custom_call_target="tpu_custom_call" | custom-call | flops 1000000000 | bytes 1312008 | tf_op jit(solution)/shard_map/pallas_call | solution.py:269
  2.4 0.0 copy-start
  2.5 18.2 %collective-permute-start = (f32[128,128]{1,0:T(8,128)S(1)}, f32[128,128]{1,0:T(8,128)S(1)}, u32[]{:S(2)}, u32[]{:S(2)}) collective-permute-start(f32[128,128]{1,0:T(8,128)S(1)} %get-tuple-element.22), channel_id=1, source_target_pairs={{0,512},{16,528},{32,544},{48,560},{64,576},{80,592},{96,608},{112... | collective-permute-start | bytes 196616 | tf_op jit(solution)/shard_map/ppermute | solution.py:314
  20.6 6.1 %shard_map.56 = (f32[256,256]{1,0:T(8,128)S(1)}, f32[256,256]{1,0:T(8,128)S(1)}) custom-call(f32[256,4096]{1,0:T(8,128)} %int_hbm.1, s32[1,64]{1,0:T(1,128)} %bitcast.9), custom_call_target="tpu_custom_call" | custom-call | flops 4000000000 | bytes 4718848 | tf_op jit(solution)/shard_map/pallas_call | solution.py:269
  26.8 0.0 collective-permute-done.hop_ref
  26.8 0.7 shard_map.57
  27.5 9.7 %all-to-all-start = ((f32[32,8,128]{2,1,0:T(8,128)}), f32[32,8,128]{2,1,0:T(8,128)S(1)}, u32[]{:S(2)}, u32[]{:S(2)}) async-start(f32[32,8,128]{2,1,0:T(8,128)} %bitcast.2), calls=%async_computation | async-start | bytes 262144 | tf_op jit(solution)/shard_map/all_to_all | solution.py:330
  37.1 2.2 %collective-permute-start.2 = (f32[256,256]{1,0:T(8,128)S(1)}, f32[256,256]{1,0:T(8,128)S(1)}, u32[]{:S(2)}, u32[]{:S(2)}) collective-permute-start(f32[256,256]{1,0:T(8,128)S(1)} %get-tuple-element.24), channel_id=1, source_target_pairs={{0,2},{1,3},{2,0},{3,1},{4,6},{5,7},{6,4},{7,5},{8,10},{9,11},{10,... | collective-permute-start | bytes 786440 | tf_op jit(solution)/shard_map/ppermute | solution.py:300
  39.3 7.0 %all-to-all-done = f32[32,8,128]{2,1,0:T(8,128)S(1)} async-done(((f32[32,8,128]{2,1,0:T(8,128)}), f32[32,8,128]{2,1,0:T(8,128)S(1)}, u32[]{:S(2)}, u32[]{:S(2)}) %all-to-all-start) | async-done | bytes 131104 | tf_op jit(solution)/shard_map/all_to_all | solution.py:330
  46.3 0.1 shard_map.58.one_ref
  46.4 2.2 %collective-permute-start.1 = (f32[128,256]{1,0:T(8,128)S(1)}, f32[128,256]{1,0:T(8,128)S(1)}, u32[]{:S(2)}, u32[]{:S(2)}) collective-permute-start(f32[128,256]{1,0:T(8,128)S(1)} %shard_map.58.one_ref), channel_id=1, source_target_pairs={{0,2},{1,3},{2,0},{3,1},{4,6},{5,7},{6,4},{7,5},{8,10},{9,11},{10,... | collective-permute-start | bytes 393224 | tf_op jit(solution)/shard_map/ppermute | solution.py:300
  48.6 0.0 collective-permute-done.2.got_ref
  48.7 3.5 %collective-permute-done.1.two_ref = f32[128,256]{1,0:T(8,128)S(1)} collective-permute-done((f32[128,256]{1,0:T(8,128)S(1)}, f32[128,256]{1,0:T(8,128)S(1)}, u32[]{:S(2)}, u32[]{:S(2)}) %collective-permute-start.1) | collective-permute-done | bytes 131104 | tf_op jit(solution)/shard_map/ppermute | solution.py:300
  52.2 0.0 copy-done
  52.2 1.1 %shard_map.59 = (f32[4,128,256]{2,1,0:T(8,128)S(1)}, f32[4,128,256]{2,1,0:T(8,128)S(1)}) custom-call(f32[128,256]{1,0:T(8,128)S(1)} %shard_map.58.one_ref, f32[128,256]{1,0:T(8,128)S(1)} %collective-permute-done.1.two_ref, f32[256,256]{1,0:T(8,128)S(1)} %get-tuple-element.23.keep_ref, f32[256,256]{1,0:T(8,128)S(1)} %collective-permute-done.2.got_ref, ...), custom_call_target="tpu_custom_call" | custom-call | flops 2000000000 | bytes 1836032 | tf_op jit(solution)/shard_map/pallas_call | solution.py:269
  53.3 5.4 %collective-permute-start.3 = (f32[4,128,256]{2,1,0:T(8,128)S(1)}, f32[4,128,256]{2,1,0:T(8,128)S(1)}, u32[]{:S(2)}, u32[]{:S(2)}) collective-permute-start(f32[4,128,256]{2,1,0:T(8,128)S(1)} %get-tuple-element.26), channel_id=1, source_target_pairs={{0,1},{1,0},{2,3},{3,2},{4,5},{5,4},{6,7},{7,6},{8,9},{9,8},{10,11... | collective-permute-start | bytes 1572872 | tf_op jit(solution)/shard_map/ppermute | solution.py:300
  58.7 1.5 %collective-permute-done.3.mate_ref = f32[4,128,256]{2,1,0:T(8,128)S(1)} collective-permute-done((f32[4,128,256]{2,1,0:T(8,128)S(1)}, f32[4,128,256]{2,1,0:T(8,128)S(1)}, u32[]{:S(2)}, u32[]{:S(2)}) %collective-permute-start.3) | collective-permute-done | bytes 524320 | tf_op jit(solution)/shard_map/ppermute | solution.py:300
  60.2 0.1 shard_map.60
  60.3 4.0 %collective-permute-start.4 = (f32[128,256]{1,0:T(8,128)S(1)}, f32[128,256]{1,0:T(8,128)S(1)}, u32[]{:S(2)}, u32[]{:S(2)}) collective-permute-start(f32[128,256]{1,0:T(8,128)S(1)} %get-tuple-element.30), channel_id=1, source_target_pairs={{0,4},{1,5},{2,6},{3,7},{4,0},{5,1},{6,2},{7,3},{8,12},{9,13},{10,... | collective-permute-start | bytes 393224 | tf_op jit(solution)/shard_map/ppermute | solution.py:300
  64.3 6.0 %collective-permute-done.4.got_ref = f32[128,256]{1,0:T(8,128)S(1)} collective-permute-done((f32[128,256]{1,0:T(8,128)S(1)}, f32[128,256]{1,0:T(8,128)S(1)}, u32[]{:S(2)}, u32[]{:S(2)}) %collective-permute-start.4) | collective-permute-done | bytes 131104 | tf_op jit(solution)/shard_map/ppermute | solution.py:300
  70.3 0.0 copy-start.1
  70.4 5.0 %collective-permute-start.5 = (f32[128,256]{1,0:T(8,128)S(1)}, f32[128,256]{1,0:T(8,128)S(1)}, u32[]{:S(2)}, u32[]{:S(2)}) collective-permute-start(f32[128,256]{1,0:T(8,128)S(1)} %shard_map.62), channel_id=1, source_target_pairs={{0,4},{1,5},{2,6},{3,7},{4,0},{5,1},{6,2},{7,3},{8,12},{9,13},{10,... | collective-permute-start | bytes 393224 | tf_op jit(solution)/shard_map/ppermute | solution.py:300
  75.4 5.5 %collective-permute-start.6 = (f32[128,256]{1,0:T(8,128)S(1)}, f32[128,256]{1,0:T(8,128)S(1)}, u32[]{:S(2)}, u32[]{:S(2)}) collective-permute-start(f32[128,256]{1,0:T(8,128)S(1)} %shard_map.61.after_ref), channel_id=1, source_target_pairs={{0,8},{1,9},{2,10},{3,11},{4,12},{5,13},{6,14},{7,15},{8,0},{9,1},... | collective-permute-start | bytes 393224 | tf_op jit(solution)/shard_map/ppermute | solution.py:300
  80.9 0.0 collective-permute-done.5.near_ref
  80.9 12.0 %collective-permute-done.6.far_ref = f32[128,256]{1,0:T(8,128)S(1)} collective-permute-done((f32[128,256]{1,0:T(8,128)S(1)}, f32[128,256]{1,0:T(8,128)S(1)}, u32[]{:S(2)}, u32[]{:S(2)}) %collective-permute-start.6) | collective-permute-done | bytes 131104 | tf_op jit(solution)/shard_map/ppermute | solution.py:300
  93.0 0.0 copy-done.1
  93.0 1.7 %shard_map.63 = f32[1024,256]{1,0:T(8,128)} custom-call(f32[128,256]{1,0:T(8,128)S(1)} %get-tuple-element.27.own_ref, f32[128,256]{1,0:T(8,128)S(1)} %collective-permute-done.5.near_ref, f32[128,256]{1,0:T(8,128)S(1)} %collective-permute-done.6.far_ref, s32[1,256]{1,0:T(1,128)S(1)} %bitcast.7, s32[1,64]{1,0:T(1,128)S(1)} %bitcast.10), custom_call_target="tpu_custom_call" | custom-call | flops 1000000000 | bytes 1443072 | tf_op jit(solution)/shard_map/pallas_call | solution.py:269
  (2 shorter events, 0.0 us)
Async XLA Ops:
  2.4 49.7 %copy-start = (s32[256]{0:T(256)S(1)}, s32[256]{0:T(256)}, u32[]{:S(2)}) copy-start(s32[256]{0:T(256)} %param.7) | copy-start | bytes 3076
  2.5 24.3 %collective-permute-start = (f32[128,128]{1,0:T(8,128)S(1)}, f32[128,128]{1,0:T(8,128)S(1)}, u32[]{:S(2)}, u32[]{:S(2)}) collective-permute-start(f32[128,128]{1,0:T(8,128)S(1)} %get-tuple-element.22), channel_id=1, source_target_pairs={{0,512},{16,528},{32,544},{48,560},{64,576},{80,592},{96,608},{112... | collective-permute-start | bytes 196616 | tf_op jit(solution)/shard_map/ppermute | solution.py:314
  27.5 18.8 %all-to-all-start = ((f32[32,8,128]{2,1,0:T(8,128)}), f32[32,8,128]{2,1,0:T(8,128)S(1)}, u32[]{:S(2)}, u32[]{:S(2)}) async-start(f32[32,8,128]{2,1,0:T(8,128)} %bitcast.2), calls=%async_computation | async-start | bytes 262144 | tf_op jit(solution)/shard_map/all_to_all | solution.py:330
  37.1 11.5 %collective-permute-start.2 = (f32[256,256]{1,0:T(8,128)S(1)}, f32[256,256]{1,0:T(8,128)S(1)}, u32[]{:S(2)}, u32[]{:S(2)}) collective-permute-start(f32[256,256]{1,0:T(8,128)S(1)} %get-tuple-element.24), channel_id=1, source_target_pairs={{0,2},{1,3},{2,0},{3,1},{4,6},{5,7},{6,4},{7,5},{8,10},{9,11},{10,... | collective-permute-start | bytes 786440 | tf_op jit(solution)/shard_map/ppermute | solution.py:300
  46.4 5.7 %collective-permute-start.1 = (f32[128,256]{1,0:T(8,128)S(1)}, f32[128,256]{1,0:T(8,128)S(1)}, u32[]{:S(2)}, u32[]{:S(2)}) collective-permute-start(f32[128,256]{1,0:T(8,128)S(1)} %shard_map.58.one_ref), channel_id=1, source_target_pairs={{0,2},{1,3},{2,0},{3,1},{4,6},{5,7},{6,4},{7,5},{8,10},{9,11},{10,... | collective-permute-start | bytes 393224 | tf_op jit(solution)/shard_map/ppermute | solution.py:300
  53.3 6.9 %collective-permute-start.3 = (f32[4,128,256]{2,1,0:T(8,128)S(1)}, f32[4,128,256]{2,1,0:T(8,128)S(1)}, u32[]{:S(2)}, u32[]{:S(2)}) collective-permute-start(f32[4,128,256]{2,1,0:T(8,128)S(1)} %get-tuple-element.26), channel_id=1, source_target_pairs={{0,1},{1,0},{2,3},{3,2},{4,5},{5,4},{6,7},{7,6},{8,9},{9,8},{10,11... | collective-permute-start | bytes 1572872 | tf_op jit(solution)/shard_map/ppermute | solution.py:300
  60.3 10.0 %collective-permute-start.4 = (f32[128,256]{1,0:T(8,128)S(1)}, f32[128,256]{1,0:T(8,128)S(1)}, u32[]{:S(2)}, u32[]{:S(2)}) collective-permute-start(f32[128,256]{1,0:T(8,128)S(1)} %get-tuple-element.30), channel_id=1, source_target_pairs={{0,4},{1,5},{2,6},{3,7},{4,0},{5,1},{6,2},{7,3},{8,12},{9,13},{10,... | collective-permute-start | bytes 393224 | tf_op jit(solution)/shard_map/ppermute | solution.py:300
  70.3 22.6 %copy-start.1 = (s32[64]{0:T(128)S(1)}, s32[64]{0:T(128)}, u32[]{:S(2)}) copy-start(s32[64]{0:T(128)} %param.8) | copy-start | bytes 772
  70.4 10.6 %collective-permute-start.5 = (f32[128,256]{1,0:T(8,128)S(1)}, f32[128,256]{1,0:T(8,128)S(1)}, u32[]{:S(2)}, u32[]{:S(2)}) collective-permute-start(f32[128,256]{1,0:T(8,128)S(1)} %shard_map.62), channel_id=1, source_target_pairs={{0,4},{1,5},{2,6},{3,7},{4,0},{5,1},{6,2},{7,3},{8,12},{9,13},{10,... | collective-permute-start | bytes 393224 | tf_op jit(solution)/shard_map/ppermute | solution.py:300
  75.4 17.6 %collective-permute-start.6 = (f32[128,256]{1,0:T(8,128)S(1)}, f32[128,256]{1,0:T(8,128)S(1)}, u32[]{:S(2)}, u32[]{:S(2)}) collective-permute-start(f32[128,256]{1,0:T(8,128)S(1)} %shard_map.61.after_ref), channel_id=1, source_target_pairs={{0,8},{1,9},{2,10},{3,11},{4,12},{5,13},{6,14},{7,15},{8,0},{9,1},... | collective-permute-start | bytes 393224 | tf_op jit(solution)/shard_map/ppermute | solution.py:300
